TPU v7x, 256 devices: a whole 4x4x8 slice. The times are simulated.
256 devices in a mesh: fsdp: 64 (over x_lo, z, y), tp: 4 (over x_hi, core).
Axes of the slice: x: 4 (x_hi: 2, x_lo: 2; x = x_hi * 2 + x_lo), y: 4, z: 8, core: 2. Of those that a mesh axis runs over, the one named last changes fastest.
Arguments:
- hidden: bfloat16 [16384, 4096], P('fsdp', 'tp')
- gain: float32 [4096], P('tp'), may hold values from 0.4 to 1.6
- head: bfloat16 [4096, 4096], P('fsdp', 'tp')
- targets: int32 [16384], P('fsdp'), may hold values from 0 to 4095
- row_weight: int32 [16384], P('fsdp'), may hold values from 1 to 3
Outputs:
- loss: float32 [], replicated
- grad_head: float32 [4096, 4096], P('fsdp', 'tp')
- grad_gain: float32 [4096], P('tp')
- grad_hidden: bfloat16 [16384, 4096], P('fsdp', 'tp')
All inputs are finite; a program needn't handle non-finite values.
Results may differ from a plain program's by a relative error of at most 0.0024.
The roundings to bfloat16 on the way count: a program that leaves them out, or rounds other values in their place, can miss the bound.
Values may be sent and summed in bfloat16 or wider, within the bound.
A program may use at most 64 MiB of HBM per device.

v0:
```python
import jax
import jax.numpy as jnp
from jax import lax
from jax.sharding import PartitionSpec as P

D = 4096


epsilon = 1e-05


def body(hidden, gain, head, targets, row_weight):
    width = D
    hidden_wide = hidden.astype(jnp.float32)
    row_scale = row_weight.astype(jnp.float32)
    total = lax.psum(jnp.sum(row_scale), "fsdp")
    squares = lax.psum(jnp.sum(hidden_wide * hidden_wide, axis=1), "tp")
    inverse_rms = lax.rsqrt(squares / width + epsilon)
    normed_part = (hidden_wide * inverse_rms[:, None] * gain[None, :]).astype(jnp.bfloat16)
    normed_full = lax.all_gather(normed_part, "tp", axis=1, tiled=True)
    head_full = lax.all_gather(head, "fsdp", axis=0, tiled=True)
    logits = jnp.dot(normed_full, head_full, preferred_element_type=jnp.float32)
    column_count = head.shape[1]
    column_start = lax.axis_index("tp") * column_count
    local_target = targets - column_start
    columns = jnp.arange(column_count, dtype=jnp.int32)
    target_mask = local_target[:, None] == columns[None, :]
    picked_local = jnp.sum(jnp.where(target_mask, logits, jnp.float32(0.0)), axis=1)
    local_max = jnp.max(logits, axis=1)
    largest = lax.pmax(local_max, "tp")
    expsum, picked = lax.psum(
        (jnp.sum(jnp.exp(logits - largest[:, None]), axis=1), picked_local), "tp"
    )
    lse = largest + jnp.log(expsum)
    loss_local = jnp.sum(row_scale * (lse - picked))
    probs = jnp.exp(logits - lse[:, None])
    dlogits = (row_scale[:, None] * (probs - target_mask.astype(jnp.float32))).astype(jnp.bfloat16)
    head_sum = lax.psum_scatter(
        lax.dot_general(
            normed_full, dlogits, (((0,), (0,)), ((), ())), preferred_element_type=jnp.float32
        ),
        "fsdp",
        scatter_dimension=0,
        tiled=True,
    )
    dnormed_part = lax.dot_general(
        dlogits, head_full, (((1,), (1,)), ((), ())), preferred_element_type=jnp.float32
    )
    dnormed_raw = lax.psum_scatter(dnormed_part, "tp", scatter_dimension=1, tiled=True)
    gained_raw = gain[None, :] * dnormed_raw
    rowdot_raw = lax.psum(jnp.sum(gained_raw * hidden_wide, axis=1), "tp")
    dnormed_raw, gained_raw, rowdot_raw = (dnormed_raw, gained_raw, rowdot_raw)
    gain_local = jnp.sum(dnormed_raw * hidden_wide * inverse_rms[:, None], axis=0)
    loss_sum = lax.psum(loss_local, "fsdp")
    gain_sum = lax.psum(gain_local, "fsdp")
    inverse_total = 1.0 / total
    loss = loss_sum * inverse_total
    grad_head = head_sum * inverse_total
    grad_gain = gain_sum * inverse_total
    gained = gained_raw * inverse_total
    rowdot = rowdot_raw * inverse_total
    grad_hidden = (
        inverse_rms[:, None] * gained - hidden_wide * (inverse_rms**3 * rowdot / width)[:, None]
    )
    return (loss, grad_head, grad_gain, grad_hidden.astype(jnp.bfloat16))


def solution(mesh):
    in_specs = (P("fsdp", "tp"), P("tp"), P("fsdp", "tp"), P("fsdp"), P("fsdp"))
    out_specs = (P(), P("fsdp", "tp"), P("tp"), P("fsdp", "tp"))
    return jax.shard_map(body, mesh=mesh, in_specs=in_specs, out_specs=out_specs, check_vma=False)
```

profile of v0, /device:TPU:2, one launch (start us, length us, event | category | flops | bytes accessed | tf_op | source)
XLA Modules:
  0.0 813.5 jit_solution(2882208654465605550)
XLA Ops:
  7.2 0.0 all-gather.3.cloned.1.call-start
  7.2 1.2 fusion
  8.4 9.0 %psum.49 = f32[256]{0:T(256)S(1)} all-reduce(f32[256]{0:T(256)S(1)} %fusion), channel_id=1, replica_groups=mesh['fsdp'=64,'tp'=4] {'tp'}, use_global_device_ids=true, to_apply=%region_1.0 | all-reduce | flops 256 | bytes 2048 | tf_op jit(solution)/shard_map/psum | solution.py:17
  17.5 2.0 fusion.2
  19.5 0.0 all-gather.3.cloned.1.call-update
  19.5 0.0 all-gather.5.cloned.1.call-start
  19.6 0.7 all-gather.5.cloned.1.call-update
  20.3 0.0 reduce-scatter.5.cloned.1.call-start
  20.3 0.7 convert_element_type.18
  21.0 0.7 broadcast_subtract_fusion
  21.7 28.2 %all-gather.3.cloned.1.call-done = bf16[256,4096]{1,0:T(8,128)(2,1)} async-done(((bf16[256,1024]{1,0:T(8,128)(2,1)}), bf16[256,4096]{1,0:T(8,128)(2,1)}) %all-gather.3.cloned.1.call-update) | async-done | bytes 2097168 | tf_op jit(solution)/shard_map/all_gather | solution.py:20
  49.9 313.0 %all-gather.5.cloned.1.call-done = bf16[4096,1024]{1,0:T(8,128)(2,1)} async-done(((bf16[64,1024]{1,0:T(8,128)(2,1)}), bf16[4096,1024]{1,0:T(8,128)(2,1)}) %all-gather.5.cloned.1.call-update) | async-done | bytes 8388624 | tf_op jit(solution)/shard_map/all_gather | solution.py:21
  362.9 6.4 fusion.12
  369.3 7.2 pmax.7
  376.5 0.5 select_reduce_fusion
  377.0 9.3 %psum.50 = f32[256]{0:T(256)S(1)} all-reduce(f32[256]{0:T(256)S(1)} %get-tuple-element.7), channel_id=1, replica_groups=mesh['fsdp'=64,'tp'=4] {'tp'}, use_global_device_ids=true, to_apply=%region_5.6 | all-reduce | flops 256 | bytes 2048 | tf_op jit(solution)/shard_map/psum | solution.py:31
  386.2 0.0 copy-start.1
  386.2 8.0 fusion.10
  394.2 0.0 reduce-scatter.5.cloned.1.call-update
  394.2 0.0 reduce-scatter.3.cloned.1.call-start
  394.3 0.0 copy-done.1
  394.3 8.9 %fusion.11 = f32[4096,1024]{1,0:T(8,128)} fusion(bf16[256,4096]{1,0:T(8,128)(2,1)S(1)} %copy-done.1, f32[256,1024]{1,0:T(8,128)S(1)} %get-tuple-element.16, f32[256]{0:T(256)S(1)} %log_add_fusion, f32[256]{0:T(256)S(1)} %convert_element_type.18, s32[256]{0:T(256)S(1)} %broadcast_subtract_fusion), kind=kOutput, calls=%fused_computation.28 | convolution fusion | flops 2149056512 | bytes 19926016 | tf_op jit(solution)/shard_map/dot_general | solution.py:39
  403.2 0.0 copy-start
  403.2 0.0 copy-start.2
  403.2 0.0 copy-start.3
  403.2 0.0 reduce-scatter.3.cloned.1.call-update
  403.2 44.0 %reduce-scatter.5.cloned.1.call-done = f32[256,1024]{1,0:T(8,128)} async-done(((f32[256,4096]{1,0:T(8,128)}), f32[256,1024]{1,0:T(8,128)}) %reduce-scatter.5.cloned.1.call-update) | async-done | bytes 1048592 | tf_op jit(solution)/shard_map/reduce_scatter | solution.py:49
  447.2 0.0 copy-done
  447.2 0.0 copy-done.2
  447.2 1.5 fusion.5
  448.8 8.4 %all-reduce.1 = (f32[256]{0:T(256)S(1)}, f32[256]{0:T(256)S(1)}) all-reduce(f32[256]{0:T(256)S(1)} %get-tuple-element.6, f32[256]{0:T(256)S(1)} %get-tuple-element.4), channel_id=1, replica_groups=mesh['fsdp'=64,'tp'=4] {'tp'}, use_global_device_ids=true, to_apply=%region_7.8 | all-reduce | flops 512 | bytes 4096 | tf_op jit(solution)/shard_map/psum | solution.py:31
  457.1 0.0 copy-done.3
  457.1 0.6 convert_reduce_fusion
  457.7 160.9 %all-reduce = (f32[]{:T(128)}, f32[]{:T(128)}, f32[1024]{0:T(1024)S(1)}) all-reduce(f32[]{:T(128)} %get-tuple-element.9, f32[]{:T(128)} %get-tuple-element.8, f32[1024]{0:T(1024)S(1)} %get-tuple-element.5), channel_id=1, replica_groups=mesh['fsdp'=64,'tp'=4] {'fsdp'}, use_global_device_ids=true, to_apply=%region_9.10 | all-reduce | flops 1026 | bytes 8208 | tf_op jit(solution)/shard_map/psum | solution.py:54
  620.0 0.6 broadcast_multiply_fusion.1
  620.6 2.3 fusion.7
  622.9 181.2 %reduce-scatter.3.cloned.1.call-done = f32[64,1024]{1,0:T(8,128)} async-done(((f32[4096,1024]{1,0:T(8,128)}), f32[64,1024]{1,0:T(8,128)}) %reduce-scatter.3.cloned.1.call-update) | async-done | bytes 262160 | tf_op jit(solution)/shard_map/reduce_scatter | solution.py:38
  804.1 1.7 broadcast_multiply_fusion
  (3 shorter events, 0.0 us)
Async XLA Ops:
  7.2 42.7 %all-gather.3.cloned.1.call-start = ((), (), s32[]{:S(2)}) async-start(), calls=%async_computation.2 | async-start | bytes 2621440 | tf_op jit(solution)/shard_map/all_gather | solution.py:20
  19.5 343.4 %all-gather.5.cloned.1.call-start = ((), (), s32[]{:S(2)}) async-start(), calls=%async_computation.3 | async-start | bytes 8519680 | tf_op jit(solution)/shard_map/all_gather | solution.py:21
  20.3 426.9 %reduce-scatter.5.cloned.1.call-start = ((), (), s32[]{:S(2)}) async-start(), calls=%async_computation.5 | async-start | bytes 5242880 | tf_op jit(solution)/shard_map/reduce_scatter | solution.py:49
  386.2 8.1 copy-start.1
  394.2 409.9 %reduce-scatter.3.cloned.1.call-start = ((), (), s32[]{:S(2)}) async-start(), calls=%async_computation.4 | async-start | bytes 17039360 | tf_op jit(solution)/shard_map/reduce_scatter | solution.py:38
  403.2 44.0 %copy-start = (bf16[256,1024]{1,0:T(8,128)(2,1)S(1)}, bf16[256,1024]{1,0:T(8,128)(2,1)}, u32[]{:S(2)}) copy-start(bf16[256,1024]{1,0:T(8,128)(2,1)} %param.5) | copy-start | bytes 1572868
  403.2 44.0 %copy-start.2 = (f32[1024]{0:T(1024)S(1)}, f32[1024]{0:T(1024)}, u32[]{:S(2)}) copy-start(f32[1024]{0:T(1024)} %param.6) | copy-start | bytes 12292
  403.2 53.9 %copy-start.3 = (s32[256]{0:T(256)S(1)}, s32[256]{0:T(256)}, u32[]{:S(2)}) copy-start(s32[256]{0:T(256)} %param.9) | copy-start | bytes 3076
Sparse Core Ops, SparseCore 0:
  19.6 30.2 all-gather.2
  51.7 311.1 all-gather.4
  394.3 52.8 reduce-scatter.4
  449.8 354.2 reduce-scatter.2
where the time goes:
time: 814 us; the launch traced here: 813 us
  waiting for transfers between devices  567 us (70%)
  blocking collectives  195 us (24%)
  matrix products  23.3 us (3%)
  between operations  16.3 us (2%)
  other arithmetic  11.8 us (1%)
    all_gather x1, waiting for transfers between devices, body(): head_full = lax.all_gather(head, 'fsdp', axis=0, tiled=True)  313 us
    reduce_scatter x1, waiting for transfers between devices, body(): lax.psum_scatter(lax.dot_general(normed_full, dlogits, (((0,), (0,)), (()...  181 us
    psum x1, blocking collectives, body(): loss_sum = lax.psum(loss_local, 'fsdp')  161 us
    reduce_scatter x1, waiting for transfers between devices, body(): lax.psum_scatter(dnormed_part, 'tp', scatter_dimension=1, tiled=True)  44 us
    all_gather x1, waiting for transfers between devices, body(): normed_full = lax.all_gather(normed_part, 'tp', axis=1, tiled=True)  28.2 us
    psum x2, blocking collectives, body(): lax.psum((jnp.sum(jnp.exp(logits - largest[:, None]), axis=1), picked_loc...  17.6 us
  transfers between devices with their start and end apart: 4, of which 4 were waited for; matrix products, arithmetic and copies ran while one was open for 2% of the time, Pallas kernels for 0%

commit v1 on v0

v1 whole, which is shorter than its diff:
```python
import functools

import jax
import jax.numpy as jnp
from jax import lax
from jax.experimental import pallas as pl
from jax.experimental.pallas import tpu as pltpu
from jax.sharding import PartitionSpec as P

D = 4096
EPS = 1e-05
MESH = pl.DeviceIdType.MESH
F32 = jnp.float32
BF16 = jnp.bfloat16

DY = (1, 3, 2)
SZ = (1, 7)
PEERS = ((1, 0), (3, 0), (2, 0), (0, 1), (1, 1), (3, 1), (2, 1))
FAR_Z = (4, 3, 5, 2, 6, 1, 7, 0)
NEAR_Z = (0, 7, 1, 6, 2, 5, 3, 4)


def kernel(
    hid, gain, hin, tgt, wgt,
    o_loss, o_gh, o_gg, o_hid,
    hb, xg, nm, gg4, tw, ssq, invb, tgtb, wb, lg, dl, dlt,
    st, qt, lseb, stat,
    ght, sba, rba, sa2, ra2, sbb, rbb, syb, ryb, fa, fb, ghs, ghr,
    dno, dns, dnr, dxs, dxr, rbx, tsum2, gps, gxr, msg, ary, arz, tsum, tot_y, tot_z,
    xh_s, xh_r, tw_s, tw_r, gn_s, gn_r, hx_s, hx_r, hf_s, hf_r,
    az_s, az_r, ay_s, ay_r, by_s, by_r, bz_s, bz_r,
    st_s, st_r, qt_s, qt_r, ty_s, ty_r, tz_s, tz_r,
    ra_s, ra_r, rz_s, rz_r, rb_s, rb_r, ry_s, ry_r, fx_s, fx_r,
    dc_s, dc_r, dx_s, dx_r, gx_s, gx_r, gy_s, gy_r, gz_s, gz_r,
):
    f = lax.axis_index("fsdp")
    t = lax.axis_index("tp")
    xl = f // 32
    z = (f // 4) % 8
    y = f % 4
    xh = t // 2
    c = t % 2
    x = xh * 2 + xl

    def dev(x_, y_, z_, c_):
        return (((x_ % 2) * 8 + z_) * 4 + y_, (x_ // 2) * 2 + c_)

    def at_x(dx, dc=0):
        return dev((x + dx) % 4, y, z, (c + dc) % 2)

    def at_y(dy):
        return dev(x, (y + dy) % 4, z, c)

    def at_z(dz):
        return dev(x, y, (z + dz) % 8, c)

    mate = dev(xh * 2 + (1 - xl), y, z, c)

    def yy(k):
        return (y + k) % 4

    def zz(k):
        return (z + k) % 8

    partners = [at_x(dx, dc) for dx, dc in PEERS] + [at_y(d) for d in DY] + [at_z(d) for d in range(1, 8)]
    barrier = pltpu.get_barrier_semaphore()
    for p in partners:
        pl.semaphore_signal(barrier, inc=1, device_id=p, device_id_type=MESH)
    pl.semaphore_wait(barrier, len(partners))

    sent = []

    def rc(src, dst, ss, rs, to):
        return pltpu.make_async_remote_copy(
            src_ref=src, dst_ref=dst, send_sem=ss, recv_sem=rs, device_id=to, device_id_type=MESH
        )

    def send(src, dst, ss, rs, to):
        cp = rc(src, dst, ss, rs, to)
        cp.start()
        sent.append(cp)

    def got(dst, rs):
        rc(dst, dst, rs, rs, at_y(1)).wait_recv()

    oth = pl.multiple_of((1 - xl) * 512, 512)
    own = pl.multiple_of(xl * 512, 512)
    send(hin.at[:, pl.ds(oth, 512)], hb.at[z, y, xl], xh_s, xh_r, mate)
    hb[z, y, xl] = hin[:, pl.ds(own, 512)]

    def b_hop(s, d, k, yk):
        ref = hb.at[zz(-SZ[s] * d), yk, xl]
        send(ref, ref, bz_s.at[s, d, k], bz_r.at[s, d, k], at_z(SZ[s]))

    for j in range(3):
        ref = hb.at[z, y, xl]
        send(ref, ref, by_s.at[j], by_r.at[j], at_y(DY[j]))
    for s in range(2):
        b_hop(s, 0, 0, y)

    tw[xl, 0:2, :] = tgt[...].astype(F32)
    tw[xl, 2:4, :] = wgt[...].astype(F32)
    send(tw.at[xl], tw.at[xl], tw_s, tw_r, mate)
    gg4[t] = gain[...]
    GP = ((0, 1), (2, 0), (2, 1))
    for i, (dx, dc) in enumerate(GP):
        send(gg4.at[t], gg4.at[t], gn_s.at[i], gn_r.at[i], at_x(dx, dc))

    for i, (dx, dc) in enumerate(((1, 0), (3, 0), (2, 0), (0, 1))):
        send(hid, xg.at[xl, t], hx_s.at[i], hx_r.at[i], at_x(dx, dc))
    xg[xl, t] = hid[...]

    def a_hop(s, d):
        ref = hb.at[zz(-SZ[s] * d), y, 1 - xl]
        send(ref, ref, az_s.at[s, d], az_r.at[s, d], at_z(SZ[s]))

    def a_out(k):
        ref = hb.at[zz(k), y, 1 - xl]
        for j in range(3):
            send(ref, ref, ay_s.at[k, j], ay_r.at[k, j], at_y(DY[j]))

    def ywas(j):
        return yy(-DY[j])

    for j in range(3):
        ref = hb.at[z, ywas(j), xl]
        got(ref, by_r.at[j])
        for s in range(2):
            b_hop(s, 0, j + 1, ywas(j))
    got(hb.at[z, y, 1 - xl], xh_r)
    a_hop(0, 0)
    a_hop(1, 0)
    a_out(0)

    got(tw.at[1 - xl], tw_r)

    def ssq_block(xl_, t_):
        def step(i, carry):
            rows = pl.ds(i * 32, 32)
            v = xg[xl_, t_, rows, :].astype(F32)
            v = v * v
            acc = v[:, 0:128]
            for k in range(1, 8):
                acc = acc + v[:, k * 128:(k + 1) * 128]
            ssq[xl_, rows, :] += acc
            return carry
        lax.fori_loop(0, 8, step, 0)

    ssq[...] = jnp.zeros_like(ssq)
    ssq_block(xl, t)

    w_all = tw[0, 2:4, :] + tw[1, 2:4, :]
    tsum[...] = jnp.zeros_like(tsum)
    tsum[0:2, :] = w_all
    for j in range(3):
        send(tsum, tot_y.at[j], ty_s.at[j], ty_r.at[j], at_y(DY[j]))

    def col(row):
        return jnp.transpose(jnp.broadcast_to(row, (128, 128)))

    for a in range(2):
        for k in range(2):
            tgtb[a, k * 128:(k + 1) * 128, :] = col(tw[a, k:k + 1, :])
            wb[a, k * 128:(k + 1) * 128, :] = col(tw[a, 2 + k:3 + k, :])

    def limit(s, k):
        if k < 0:
            return 4 if s == 0 else 3
        return 4 if (k < 2) == (s == 0) else 3

    def a_arrive(s, d):
        got(hb.at[zz(-SZ[s] * d), y, 1 - xl], az_r.at[s, d - 1])
        if d < limit(s, -1):
            a_hop(s, d)
        a_out((-SZ[s] * d) % 8)

    def b_arrive(s, d, k):
        yk = y if k == 0 else ywas(k - 1)
        got(hb.at[zz(-SZ[s] * d), yk, xl], bz_r.at[s, d - 1, k])
        if d < limit(s, k):
            b_hop(s, d, k, yk)

    def b_arrivals(d):
        for k in range(4):
            for s in range(2):
                if d <= limit(s, k):
                    b_arrive(s, d, k)

    a_arrive(0, 1)
    a_arrive(1, 1)
    b_arrivals(1)
    a_arrive(0, 2)
    a_arrive(1, 2)
    for j in range(3):
        got(tot_y.at[j], ty_r.at[j])
    tsum2[...] = tsum[...] + tot_y[0] + tot_y[1] + tot_y[2]
    for d in range(1, 8):
        send(tsum2, tot_z.at[d - 1], tz_s.at[d - 1], tz_r.at[d - 1], at_z(d))
    b_arrivals(2)
    a_arrive(0, 3)
    a_arrive(1, 3)
    a_arrive(0, 4)

    XD = (1, 3, 2)

    def xblock(i):
        xs = (x - XD[i] + 4) % 4
        return xs % 2, (xs // 2) * 2

    def x_forward(i):
        a, b = xblock(i)
        ref = xg.at[a, b + c]
        got(ref, hx_r.at[i])
        send(ref, ref, hf_s.at[i], hf_r.at[i], at_x(0, 1))
        ssq_block(a, b + c)

    def x_second(i):
        a, b = xblock(i)
        got(xg.at[a, b + 1 - c], hf_r.at[i])
        ssq_block(a, b + 1 - c)

    got(xg.at[xl, xh * 2 + 1 - c], hx_r.at[3])
    ssq_block(xl, xh * 2 + 1 - c)
    b_arrivals(3)
    for i in range(3):
        x_forward(i)
    for i in range(3):
        x_second(i)
    for i, (dx, dc) in enumerate(GP):
        ts = ((xh + (dx // 2)) % 2) * 2 + (c + dc) % 2
        got(gg4.at[ts], gn_r.at[i])

    for a in range(2):
        s_ = jnp.sum(ssq[a], axis=1, keepdims=True)
        invb[a] = jnp.broadcast_to(lax.rsqrt(s_ * (1.0 / D) + EPS), (256, 128))

    def norm_z(zb):
        t0 = zb // 4
        off = (zb % 4) * 256

        def step(i, carry):
            a = i // 8
            r = pl.multiple_of((i % 8) * 32, 32)
            rows = pl.ds(r, 32)
            inv = invb[a, rows, :]
            low = lax.broadcasted_iota(jnp.int32, (32, 128), 1) < 64
            for p in range(2):
                cols = slice(off + p * 128, off + (p + 1) * 128)
                u = xg[a, t0, rows, cols].astype(F32) * inv * gg4[t0, :, cols]
                v = xg[a, t0 + 2, rows, cols].astype(F32) * inv * gg4[t0 + 2, :, cols]
                ur = pltpu.roll(u, 64, 1)
                vr = pltpu.roll(v, 64, 1)
                out = pl.ds(pl.multiple_of(i * 32, 32), 32)
                nm[zb, out, (2 * p) * 128:(2 * p + 1) * 128] = jnp.where(low, u, vr).astype(BF16)
                nm[zb, out, (2 * p + 1) * 128:(2 * p + 2) * 128] = jnp.where(low, ur, v).astype(BF16)
            return carry
        lax.fori_loop(0, 16, step, 0)

    for zb in range(8):
        norm_z(zb)

    for n, k in enumerate(NEAR_Z):
        for j in range(3):
            got(hb.at[zz(k), ywas(j), 1 - xl], ay_r.at[k, j])
        if k == 4:
            b_arrivals(4)
        part = jnp.dot(nm[zz(k)], hb[zz(k)].reshape(512, 512), preferred_element_type=F32)
        if n == 0:
            lg[...] = part
        else:
            lg[...] += part

    col0 = (t * 1024 + xl * 512).astype(F32)
    me = x * 2 + c

    def stat_step(i, carry):
        rows = pl.ds(pl.multiple_of(i * 64, 64), 64)
        l = lg[rows, :]
        m = jnp.max(l, axis=1, keepdims=True)
        e = jnp.sum(jnp.exp(l - m), axis=1, keepdims=True)
        a = i // 4
        tb = tgtb[a, pl.ds(pl.multiple_of((i % 4) * 64, 64), 64), :][:, 0:1] - col0
        cols = lax.broadcasted_iota(jnp.int32, (64, 512), 1).astype(F32)
        pk = jnp.sum(jnp.where(cols == tb, l, 0.0), axis=1, keepdims=True)
        lane = lax.broadcasted_iota(jnp.int32, (64, 128), 1)
        stat[rows, :] = jnp.where(lane == 0, m, jnp.where(lane == 1, e, jnp.where(lane == 2, pk, 0.0)))
        return carry

    lax.fori_loop(0, 8, stat_step, 0)
    for k in range(4):
        st[me, k] = jnp.transpose(stat[k * 128:(k + 1) * 128, :])[0:8, :]
    for i, (dx, dc) in enumerate(PEERS):
        send(st.at[me], st.at[me], st_s.at[i], st_r.at[i], at_x(dx, dc))

    def peer_was(i):
        dx, dc = PEERS[i]
        return ((x - dx + 4) % 4) * 2 + (c + dc) % 2

    for i in range(7):
        got(st.at[peer_was(i)], st_r.at[i])
    allst = st[...]
    mx = jnp.max(allst[:, :, 0:1, :], axis=0)
    es = jnp.sum(allst[:, :, 1:2, :] * jnp.exp(allst[:, :, 0:1, :] - mx[None]), axis=0)
    pk = jnp.sum(allst[:, :, 2:3, :], axis=0)
    lse = mx + jnp.log(es)
    loss_row = jnp.zeros((1, 128), F32)
    for k in range(4):
        loss_row = loss_row + tw[k // 2, 2 + k % 2:3 + k % 2, :] * (lse[k] - pk[k])
        lseb[k * 128:(k + 1) * 128, :] = col(lse[k])

    def dl_step(i, carry):
        a = i // 8
        r = pl.multiple_of((i % 8) * 32, 32)
        rows = pl.ds(r, 32)
        g = pl.ds(pl.multiple_of(i * 32, 32), 32)
        l = lg[g, :]
        tb = tgtb[a, rows, :][:, 0:1] - col0
        w = wb[a, rows, :][:, 0:1]
        cols = lax.broadcasted_iota(jnp.int32, (32, 512), 1).astype(F32)
        p = jnp.exp(l - lseb[g, :][:, 0:1])
        d = (w * (p - jnp.where(cols == tb, 1.0, 0.0))).astype(BF16)
        dl[a, rows, :] = d
        q = jnp.sum(d.astype(F32) * l, axis=1, keepdims=True)
        stat[g, :] = jnp.broadcast_to(q, (32, 128))
        return carry

    lax.fori_loop(0, 16, dl_step, 0)
    for a in range(2):
        dlt[:, a * 256:(a + 1) * 256] = jnp.transpose(dl[a])

    def head_grad(k):
        g = jnp.dot(dlt[...], nm[zz(k)], preferred_element_type=F32)
        for b in range(4):
            ght[k, b] = g[:, b * 128:(b + 1) * 128]
        for j in range(3):
            sba[k, j] = ght[k, yy(DY[j]), 0:256, :].astype(BF16)
            send(sba.at[k, j], rba.at[k, j], ra_s.at[k, j], ra_r.at[k, j], at_y(DY[j]))

    def qrows(q):
        return slice(256 + q * 128, 384 + q * 128)

    def b_chain(s, d, q):
        k = (SZ[s] * d) % 8
        v = ght[k, :, qrows(q), :]
        if d < (4 if q == s else 3):
            got(rbb.at[s, q, d], rb_r.at[s, q, d])
            v = v + rbb[s, q, d].astype(F32)
        sbb[s, q, d - 1] = v.astype(BF16)
        send(sbb.at[s, q, d - 1], rbb.at[s, q, d - 1], rb_s.at[s, q, d - 1], rb_r.at[s, q, d - 1], at_z(SZ[s]))

    def a_sum(k):
        v = ght[k, y, 0:256, :]
        for j in range(3):
            got(rba.at[k, j], ra_r.at[k, j])
            v = v + rba[k, j].astype(F32)
        return v

    def a_chain4():
        fa[...] = a_sum(4)
        for s in range(2):
            h = slice(s * 128, (s + 1) * 128)
            sa2[s, 3, h] = fa[h, :]
            send(sa2.at[s, 3, h], ra2.at[s, 3, h], rz_s.at[s, 3], rz_r.at[s, 3], at_z(SZ[s]))

    def a_chain(s, d):
        v = a_sum((SZ[s] * d) % 8)
        if d == 3:
            h = slice(s * 128, (s + 1) * 128)
            sa2[s, 2] = v
            got(ra2.at[s, 3, h], rz_r.at[s, 3])
            sa2[s, 2, h] = v[h] + ra2[s, 3, h]
        else:
            got(ra2.at[s, d], rz_r.at[s, d])
            sa2[s, d - 1] = v + ra2[s, d]
        send(sa2.at[s, d - 1], ra2.at[s, d - 1], rz_s.at[s, d - 1], rz_r.at[s, d - 1], at_z(SZ[s]))

    XO = (2, 1, 3, 0)

    def xdest(n):
        xs = (x + XO[n]) % 4
        return xs % 2, xs // 2

    def dn_part(out, n, cc):
        a, b = xdest(n)
        for i in range(4):
            h = hb[4 * cc + i, :, b].reshape(256, 512)
            out[n, :, i * 256:(i + 1) * 256] = lax.dot_general(
                dl[a], h, (((1,), (1,)), ((), ())), preferred_element_type=F32
            )

    def dn_start(n):
        dn_part(dns, n, 1 - c)
        send(dns.at[n], dnr.at[n], dc_s.at[n], dc_r.at[n], at_x(0, 1))
        dn_part(dno, n, c)

    def dn_sum(n):
        got(dnr.at[n], dc_r.at[n])
        a, b = xdest(n)
        tx = b * 2 + c

        def step(i, acc):
            rows = pl.ds(pl.multiple_of(i * 16, 16), 16)
            s_ = dno[n, rows, :] + dnr[n, rows, :]
            dno[n, rows, :] = s_
            if XO[n] == 2:
                dxs[rows, :] = s_.astype(BF16)
            xv = xg[a, tx, rows, :].astype(F32) * invb[a, rows, :][:, 0:1]
            pr = s_ * xv
            return acc + pr[0:8] + pr[8:16]
        acc = lax.fori_loop(0, 16, step, jnp.zeros((8, 1024), F32))
        gps[b * 2 + a] = jnp.sum(acc, axis=0, keepdims=True)
        if XO[n] == 2:
            send(dxs, dxr, dx_s.at[2], dx_r.at[2], at_x(2))
        elif XO[n] == 1:
            send(dno.at[n], rbx.at[0], dx_s.at[0], dx_r.at[0], at_x(1))
        elif XO[n] == 3:
            send(dno.at[n], rbx.at[1], dx_s.at[1], dx_r.at[1], at_x(3))

    dn_start(0)
    head_grad(4)
    b_chain(0, 4, 0)
    b_chain(1, 4, 1)
    dn_sum(0)
    head_grad(3)
    b_chain(0, 3, 1)
    head_grad(5)
    b_chain(1, 3, 0)
    dn_start(1)
    dn_start(2)
    a_chain4()
    dn_sum(1)
    dn_sum(2)
    head_grad(2)
    head_grad(6)
    b_chain(0, 3, 0)
    b_chain(1, 3, 1)
    head_grad(1)
    head_grad(7)
    head_grad(0)
    b_chain(0, 2, 1)
    b_chain(1, 2, 0)
    a_chain(0, 3)
    a_chain(1, 3)
    dn_start(3)
    dn_sum(3)

    def gpair(b):
        return gps[2 * b] + gps[2 * b + 1]

    for b in range(2):
        gxr[3 + b] = gpair(b)
    for i, dx in enumerate((1, 3, 2)):
        b = ((x + dx) % 4) // 2
        send(gxr.at[3 + b], gxr.at[i], gx_s.at[i], gx_r.at[i], at_x(dx))

    for k in range(4):
        qt[me, k] = jnp.transpose(stat[k * 128:(k + 1) * 128, :])[0:8, :]
    for i, (dx, dc) in enumerate(PEERS):
        send(qt.at[me], qt.at[me], qt_s.at[i], qt_r.at[i], at_x(dx, dc))

    b_chain(0, 2, 0)
    b_chain(1, 2, 1)
    for i in range(3):
        got(gxr.at[i], gx_r.at[i])
    msg[0] = gxr[3 + xh] + gxr[0] + gxr[1] + gxr[2]
    msg[1] = jnp.zeros((1, 1024), F32)
    msg[1, :, 0:128] = loss_row
    for j in range(3):
        send(msg, ary.at[j], gy_s.at[j], gy_r.at[j], at_y(DY[j]))

    b_chain(0, 1, 1)
    b_chain(1, 1, 0)
    a_chain(0, 2)
    a_chain(1, 2)
    for j in range(3):
        got(ary.at[j], gy_r.at[j])
    msg_sum = msg[...] + ary[0] + ary[1] + ary[2]
    ary[3] = msg_sum
    for d in range(1, 8):
        send(ary.at[3], arz.at[d - 1], gz_s.at[d - 1], gz_r.at[d - 1], at_z(d))
    for d in range(1, 8):
        got(tot_z.at[d - 1], tz_r.at[d - 1])
    tot = tsum2[...]
    for d in range(7):
        tot = tot + tot_z[d]
    inv_total = 1.0 / jnp.sum(jnp.sum(tot, axis=1, keepdims=True), axis=0, keepdims=True)

    for i in range(7):
        got(qt.at[peer_was(i)], qt_r.at[i])
    qsum = qt[0]
    for i in range(1, 8):
        qsum = qsum + qt[i]
    for k in range(4):
        lseb[k * 128:(k + 1) * 128, :] = col(qsum[k, 0:1, :])

    b_chain(0, 1, 0)
    b_chain(1, 1, 1)
    a_chain(0, 1)
    a_chain(1, 1)
    va = a_sum(0)
    for s in range(2):
        got(ra2.at[s, 0], rz_r.at[s, 0])
        va = va + ra2[s, 0]
    fa[...] = va
    ft = jnp.transpose(fa[...])
    for a in range(2):
        ghs[a, :, 0:256] = ft[a * 64:(a + 1) * 64]
    for q in (1, 0):
        v = ght[0, :, qrows(q), :]
        for s in range(2):
            got(rbb.at[s, q, 0], rb_r.at[s, q, 0])
            v = v + rbb[s, q, 0].astype(F32)
        syb[q] = v
        for j in range(3):
            src = syb.at[q, yy(DY[j])]
            send(src, ryb.at[q, j], ry_s.at[q, j], ry_r.at[q, j], at_y(DY[j]))
    for q in (1, 0):
        v = syb[q, y]
        for j in range(3):
            got(ryb.at[q, j], ry_r.at[q, j])
            v = v + ryb[q, j]
        fb[q] = v
        ft = jnp.transpose(fb[q])
        for a in range(2):
            ghs[a, :, 256 + q * 128:384 + q * 128] = ft[a * 64:(a + 1) * 64]
    send(ghs.at[1 - xl], ghr, fx_s, fx_r, mate)

    for d in range(1, 8):
        got(arz.at[d - 1], gz_r.at[d - 1])
    gl = ary[3]
    for d in range(7):
        gl = gl + arz[d]
    o_gg[...] = gl[0] * inv_total
    o_loss[...] = jnp.broadcast_to(jnp.sum(gl[1], axis=1, keepdims=True) * inv_total, (8, 128))
    o_gh[:, pl.ds(own, 512)] = ghs[xl] * inv_total

    got(rbx.at[0], dx_r.at[0])
    got(rbx.at[1], dx_r.at[1])
    got(dxr, dx_r.at[2])
    gt = gg4[t]

    def fin(i, carry):
        rows = pl.ds(pl.multiple_of(i * 16, 16), 16)
        qrow = pl.ds(pl.multiple_of(xl * 256 + i * 16, 16), 16)
        dn = dno[3, rows, :] + rbx[0, rows, :] + rbx[1, rows, :] + dxr[rows, :].astype(F32)
        inv = invb[xl, rows, :][:, 0:1]
        q = lseb[qrow, :][:, 0:1]
        xv = hid[rows, :].astype(F32)
        u = inv * inv_total
        o_hid[rows, :] = (dn * gt * u - xv * (inv * u * q * (1.0 / D))).astype(BF16)
        return carry

    lax.fori_loop(0, 16, fin, 0)
    got(ghr, fx_r)
    o_gh[:, pl.ds(oth, 512)] = ghr[...] * inv_total
    for cp in sent:
        cp.wait_send()


def body(hidden, gain, head, targets, row_weight):
    V = pltpu.VMEM
    S = pltpu.SemaphoreType.DMA
    vm = pl.BlockSpec(memory_space=pltpu.VMEM)
    scratch = [
        V((8, 4, 2, 64, 512), BF16),
        V((2, 4, 256, 1024), BF16),
        V((8, 512, 512), BF16),
        V((4, 1, 1024), F32),
        V((2, 8, 128), F32),
        V((2, 256, 128), F32),
        V((2, 256, 128), F32),
        V((2, 256, 128), F32),
        V((2, 256, 128), F32),
        V((512, 512), F32),
        V((2, 256, 512), BF16),
        V((512, 512), BF16),
        V((8, 4, 8, 128), F32),
        V((8, 4, 8, 128), F32),
        V((512, 128), F32),
        V((512, 128), F32),
        V((8, 4, 512, 128), F32),
        V((8, 3, 256, 128), BF16),
        V((8, 3, 256, 128), BF16),
        V((2, 4, 256, 128), F32),
        V((2, 4, 256, 128), F32),
        V((2, 2, 4, 4, 128, 128), BF16),
        V((2, 2, 4, 4, 128, 128), BF16),
        V((2, 4, 128, 128), F32),
        V((2, 3, 128, 128), F32),
        V((256, 128), F32),
        V((2, 128, 128), F32),
        V((2, 64, 512), F32),
        V((64, 512), F32),
        V((4, 256, 1024), F32),
        V((4, 256, 1024), F32),
        V((4, 256, 1024), F32),
        V((256, 1024), BF16),
        V((256, 1024), BF16),
        V((2, 256, 1024), F32),
        V((8, 128), F32),
        V((4, 1, 1024), F32),
        V((5, 1, 1024), F32),
        V((2, 1, 1024), F32),
        V((4, 2, 1, 1024), F32),
        V((7, 2, 1, 1024), F32),
        V((8, 128), F32),
        V((3, 8, 128), F32),
        V((7, 8, 128), F32),
    ]
    shapes = [
        (), (), (3,), (4,), (3,),
        (2, 4), (8, 3), (3,), (2, 4, 4),
        (7,), (7,), (3,), (7,),
        (8, 3), (2, 4), (2, 2, 4), (2, 3), (),
        (4,), (3,), (3,), (3,), (7,),
    ]
    for sh in shapes:
        scratch += [S(sh), S(sh)] if sh else [S, S]
    loss, gh, gg, gx = pl.pallas_call(
        kernel,
        out_shape=(
            jax.ShapeDtypeStruct((8, 128), F32),
            jax.ShapeDtypeStruct((64, 1024), F32),
            jax.ShapeDtypeStruct((1, 1024), F32),
            jax.ShapeDtypeStruct((256, 1024), BF16),
        ),
        in_specs=[vm] * 5,
        out_specs=(vm, vm, vm, vm),
        scratch_shapes=scratch,
        compiler_params=pltpu.CompilerParams(
            collective_id=0, has_side_effects=True, vmem_limit_bytes=62 << 20
        ),
    )(hidden, gain.reshape(1, 1024), head, targets.reshape(2, 128), row_weight.reshape(2, 128))
    return (loss[0, 0], gh, gg.reshape(1024), gx)


def solution(mesh):
    in_specs = (P("fsdp", "tp"), P("tp"), P("fsdp", "tp"), P("fsdp"), P("fsdp"))
    out_specs = (P(), P("fsdp", "tp"), P("tp"), P("fsdp", "tp"))
    return jax.shard_map(body, mesh=mesh, in_specs=in_specs, out_specs=out_specs, check_vma=False)
```

time: 814 us -> 141 us (0.17)
  waiting for transfers between devices: 567 us -> 0 us
  blocking collectives: 195 us -> 0 us
  Pallas kernels: 0 us -> 136 us
  matrix products: 23.3 us -> 0 us
  between operations: 16.3 us -> 0.65 us
  other arithmetic: 11.8 us -> 0 us
    all_gather x2 -> x0, waiting for transfers between devices: 341 us -> none  [the longest x1 313 us: body(): head_full = lax.all_gather(head, 'fsdp', axis=0, tiled=True)]
    reduce_scatter x2 -> x0, waiting for transfers between devices: 225 us -> none  [the longest x1 181 us: body(): lax.psum_scatter(lax.dot_general(normed_full, dlogits, (((0,), (0,)), (()...]
    psum x4 -> x0, blocking collectives: 188 us -> none  [the longest x1 161 us: body(): loss_sum = lax.psum(loss_local, 'fsdp')]
    pallas_call x0 -> x1, Pallas kernels: none -> 136 us  [body(): pl.pallas_call(kernel, out_shape=(jax.ShapeDtypeStruct((8, 128), F32), ja...]
    dot_general x3 -> x0, matrix products: 23.3 us -> none  [the longest x1 8.91 us: body(): lax.dot_general(normed_full, dlogits, (((0,), (0,)), ((), ())), preferred...]
  transfers between devices with their start and end apart: 4 -> 0, of which waited for: 4 -> 0; matrix products, arithmetic and copies ran while one was open for 2% -> 0% of each run, Pallas kernels for 0% -> 0%
where the time goes in v1:
time: 141 us
  Pallas kernels  136 us (96%)
  local copies, waits for them, and re-layouts  4.31 us (3%)
    pallas_call x1, Pallas kernels, body(): pl.pallas_call(kernel, out_shape=(jax.ShapeDtypeStruct((8, 128), F32), ja...  136 us
    unnamed x7, local copies, waits for them, and re-layouts  3.07 us

profile of v1, /device:TPU:2, one launch (start us, length us, event | category | flops | bytes accessed | tf_op | source)
XLA Modules:
  0.0 140.7 jit_solution(15940276911110706717)
XLA Ops:
  0.6 135.7 %shard_map.84 = (f32[8,128]{1,0:T(8,128)}, f32[64,1024]{1,0:T(8,128)}, f32[1,1024]{1,0:T(1,128)}, bf16[256,1024]{1,0:T(8,128)(2,1)}) custom-call(bf16[256,1024]{1,0:T(8,128)(2,1)} %hid.1, f32[1,1024]{1,0:T(1,128)} %bitcast.5, bf16[64,1024]{1,0:T(8,128)(2,1)} %hin.1, s32[2,128]{1,0:T(2,128)} %bitcast.7, s32[2,128]{1,0:T(2,128)} %bitcast.8), custom_call_target="tpu_custom_call" | custom-call | tf_op jit(solution)/shard_map/pallas_call | solution.py:619
  136.4 0.0 copy-start
  136.4 1.2 slice.3
  137.6 0.0 copy-start.1
  137.6 1.7 %copy.12 = f32[64,1024]{1,0:T(8,128)} copy(f32[64,1024]{1,0:T(8,128)} %get-tuple-element.17) | data formatting | bytes 524288
  139.3 0.0 copy-done.1
  139.3 0.6 copy.13
  139.9 0.0 copy-done
  139.9 0.8 copy.14
Async XLA Ops:
  136.4 3.5 %copy-start = (bf16[256,1024]{1,0:T(8,128)(2,1)S(1)}, bf16[256,1024]{1,0:T(8,128)(2,1)}, u32[]{:S(2)}) copy-start(bf16[256,1024]{1,0:T(8,128)(2,1)} %get-tuple-element.19) | copy-start | bytes 1572868
  137.6 1.7 %copy-start.1 = (f32[1,1024]{1,0:T(1,128)S(1)}, f32[1,1024]{1,0:T(1,128)}, u32[]{:S(2)}) copy-start(f32[1,1024]{1,0:T(1,128)} %get-tuple-element.10) | copy-start | bytes 12292

commit v2 on v1

v2 whole, which is shorter than its diff:
```python
import functools

import jax
import jax.numpy as jnp
from jax import lax
from jax.experimental import pallas as pl
from jax.experimental.pallas import tpu as pltpu
from jax.sharding import PartitionSpec as P

D = 4096
EPS = 1e-05
MESH = pl.DeviceIdType.MESH
F32 = jnp.float32
BF16 = jnp.bfloat16

DY = (1, 3, 2)
SZ = (1, 7)
PEERS = ((1, 0), (3, 0), (2, 0), (0, 1), (1, 1), (3, 1), (2, 1))
GATHER = (
    ("xe",), ("by", 1), ("bz", 0, 1, 0), ("bz", 1, 1, 0), ("by", 2), ("az", 0, 1), ("az", 1, 1), ("xo",),
    ("bz", 0, 1, 1), ("bz", 1, 1, 1), ("bz", 0, 2, 0), ("bz", 1, 2, 0), ("xf", 1), ("xf", 0), ("by", 3),
    ("az", 0, 2), ("az", 1, 2), ("xs", 1), ("xs", 0), ("ty",), ("bz", 0, 1, 2), ("bz", 1, 1, 2), ("iv", 1),
    ("nm", 1, 0), ("nm", 1, 1), ("nm", 1, 2), ("nm", 1, 3), ("bz", 0, 2, 1), ("bz", 1, 2, 1), ("nm", 1, 4),
    ("nm", 1, 5), ("nm", 1, 6), ("nm", 1, 7), ("bz", 0, 3, 0), ("bz", 1, 3, 0), ("az", 0, 3), ("az", 1, 3),
    ("bz", 0, 1, 3), ("bz", 1, 1, 3), ("bz", 0, 2, 2), ("bz", 1, 2, 2), ("xf", 2), ("bz", 0, 3, 1), ("bz", 1, 3, 1),
    ("tz", 1), ("xs", 2), ("iv", 0), ("nm", 0, 0), ("nm", 0, 1), ("nm", 0, 2), ("bz", 0, 4, 0), ("bz", 1, 2, 3),
    ("nm", 0, 3), ("nm", 0, 4), ("nm", 0, 5), ("az", 0, 4), ("bz", 1, 3, 2), ("nm", 0, 6), ("nm", 0, 7), ("lg", 0),
    ("bz", 0, 2, 3), ("bz", 1, 3, 3), ("lg", 7), ("lg", 1), ("bz", 0, 3, 2), ("bz", 1, 4, 2), ("lg", 6), ("tz", 2),
    ("lg", 2), ("bz", 0, 4, 1), ("lg", 3), ("bz", 0, 3, 3), ("bz", 1, 4, 3), ("lg", 5), ("lg", 4),
)
SCATTER = (
    ("hg", 4), ("bc", 0, 4, 0), ("bc", 1, 4, 1), ("bc", 0, 4, 2), ("bc", 1, 4, 3), ("hg", 3), ("bc", 0, 3, 1),
    ("bc", 0, 3, 3), ("hg", 5), ("bc", 1, 3, 0), ("bc", 1, 3, 2), ("ds", 0), ("hg", 2), ("ds", 1), ("du", 0),
    ("bc", 0, 3, 0), ("bc", 1, 3, 1), ("ds", 2), ("bc", 0, 3, 2), ("bc", 1, 3, 3), ("hg", 6), ("a4",), ("du", 1),
    ("bc", 0, 2, 1), ("bc", 1, 2, 0), ("ds", 3), ("du", 2), ("bc", 0, 2, 3), ("bc", 1, 2, 2), ("du", 3), ("gy",),
    ("hg", 1), ("bc", 0, 2, 0), ("bc", 1, 2, 1), ("hg", 7), ("hg", 0), ("xr", 1), ("xr", 2), ("ac", 0, 3),
    ("ac", 1, 3), ("bc", 0, 2, 2), ("bc", 1, 2, 3), ("bc", 0, 1, 1), ("bc", 1, 1, 0), ("tz", 3), ("bc", 0, 1, 3),
    ("bc", 1, 1, 2), ("bc", 0, 1, 0), ("bc", 1, 1, 1), ("ac", 0, 2), ("ac", 1, 2), ("gz",), ("bc", 0, 1, 2),
    ("bc", 1, 1, 3), ("tz", 4), ("qt",), ("bf", 0), ("bf", 1), ("ac", 0, 1), ("ac", 1, 1), ("bf", 2), ("bf", 3),
    ("gx",), ("bg", 0), ("bg", 1), ("af",), ("fi",), ("gf",), ("gh",),
)


def kernel(
    hid, gain, hin_hbm, tgt_hbm, wgt_hbm,
    r_loss, r_gh, r_gg, r_hid,
    tgt, wgt, o_loss, o_gh, o_gg, o_hid, hin, hb, xg, nm, gg4, tw, ssq, invb, tgtb, wb, lg, ex, dl, dlt,
    st, qt, lseb, stat,
    ght, sba, rba, sa4, ra4, sa3, ra3, sa2, ra2, sbb, rbb, syb, ryb, fa, fb, ghs, ghr,
    dno, dns, dnr, dxs, dxr, dos, dor, rbx, gps, gxs, gxr, msg, ary, arz, tsum, tsum2, tot_y, tot_z,
    in_s, out_s,
    xh_s, xh_r, tw_s, tw_r, gn_s, gn_r, hx_s, hx_r, hh_s, hh_r, hf_s, hf_r,
    az_s, az_r, ay_s, ay_r, by_s, by_r, bz_s, bz_r,
    st_s, st_r, qt_s, qt_r, ty_s, ty_r, tz_s, tz_r,
    ra_s, ra_r, rz_s, rz_r, rb_s, rb_r, ry_s, ry_r, fx_s, fx_r,
    dc_s, dc_r, d2_s, d2_r, dx_s, dx_r, do_s, do_r, gx_s, gx_r, gy_s, gy_r, gz_s, gz_r,
):
    f = lax.axis_index("fsdp")
    t = lax.axis_index("tp")
    xl = f // 32
    z = (f // 4) % 8
    y = f % 4
    xh = t // 2
    c = t % 2
    x = xh * 2 + xl

    def dev(x_, y_, z_, c_):
        return (((x_ % 2) * 8 + z_) * 4 + y_, (x_ // 2) * 2 + c_)

    def at_x(dx, dc=0):
        return dev((x + dx) % 4, y, z, (c + dc) % 2)

    def at_y(dy):
        return dev(x, (y + dy) % 4, z, c)

    def at_z(dz):
        return dev(x, y, (z + dz) % 8, c)

    mate = dev(xh * 2 + (1 - xl), y, z, c)

    def yy(k):
        return (y + k) % 4

    def zz(k):
        return (z + k) % 8

    partners = [at_x(dx, dc) for dx, dc in PEERS] + [at_y(d) for d in DY] + [at_z(d) for d in SZ]
    barrier = pltpu.get_barrier_semaphore()
    for p in partners:
        pl.semaphore_signal(barrier, inc=1, device_id=p, device_id_type=MESH)
    in_hid = pltpu.make_async_copy(hid, xg.at[xl, t], in_s.at[0])
    in_head = pltpu.make_async_copy(hin_hbm, hin, in_s.at[1])
    in_small = [
        pltpu.make_async_copy(src, dst, in_s.at[2 + i])
        for i, (src, dst) in enumerate(((tgt_hbm, tgt), (wgt_hbm, wgt), (gain, gg4.at[t])))
    ]
    in_head.start()
    in_hid.start()
    for cp in in_small:
        cp.start()
    oth = pl.multiple_of((1 - xl) * 512, 512)
    own = pl.multiple_of(xl * 512, 512)
    in_head.wait()
    hb[z, y, xl] = hin[:, pl.ds(own, 512)]
    pl.semaphore_wait(barrier, len(partners))

    sent = []

    def rc(src, dst, ss, rs, to):
        return pltpu.make_async_remote_copy(
            src_ref=src, dst_ref=dst, send_sem=ss, recv_sem=rs, device_id=to, device_id_type=MESH
        )

    def send(src, dst, ss, rs, to):
        cp = rc(src, dst, ss, rs, to)
        cp.start()
        sent.append(cp)

    def got(dst, rs):
        rc(dst, dst, rs, rs, at_y(1)).wait_recv()

    def b_hop(s, d, k):
        yk = y if k == 0 else ywas(k - 1)
        ref = hb.at[zz(-SZ[s] * d), yk, xl]
        send(ref, ref, bz_s.at[s, d, k], bz_r.at[s, d, k], at_z(SZ[s]))

    def a_hop(s, d):
        ref = hb.at[zz(-SZ[s] * d), y, 1 - xl]
        send(ref, ref, az_s.at[s, d], az_r.at[s, d], at_z(SZ[s]))

    def a_out(k):
        ref = hb.at[zz(k), y, 1 - xl]
        for j in range(3):
            send(ref, ref, ay_s.at[k, j], ay_r.at[k, j], at_y(DY[j]))

    def ywas(j):
        return yy(-DY[j])

    def limit(s, k):
        if k < 0:
            return 4 if s == 0 else 3
        return 4 if (k < 2) == (s == 0) else 3

    def ring_limit(s):
        return 4 if s == 0 else 3

    send(hin.at[:, pl.ds(oth, 512)], hb.at[z, y, xl], xh_s, xh_r, mate)
    def b_out(j):
        ref = hb.at[z, y, xl]
        send(ref, ref, by_s.at[j], by_r.at[j], at_y(DY[j]))

    b_out(0)
    b_out(1)
    for s in range(2):
        b_hop(s, 0, 0)
    for cp in in_small:
        cp.wait()
    tw[xl, 0:2, :] = tgt[...].astype(F32)
    tw[xl, 2:4, :] = wgt[...].astype(F32)
    send(tw.at[xl], tw.at[xl], tw_s, tw_r, mate)
    GP = ((0, 1), (2, 0), (2, 1))
    for i, (dx, dc) in enumerate(GP):
        send(gg4.at[t], gg4.at[t], gn_s.at[i], gn_r.at[i], at_x(dx, dc))
    in_hid.wait()
    for i, dx, dc in ((3, 0, 1), (0, 1, 0), (1, 3, 0)):
        send(xg.at[xl, t], xg.at[xl, t], hx_s.at[i], hx_r.at[i], at_x(dx, dc))

    def ssq_block(xl_, t_):
        def step(i, carry):
            rows = pl.ds(pl.multiple_of(i * 32, 32), 32)
            v = xg[xl_, t_, rows, :].astype(F32)
            v = v * v
            acc = v[:, 0:128]
            for k in range(1, 8):
                acc = acc + v[:, k * 128:(k + 1) * 128]
            ssq[xl_, rows, :] += acc
            return carry
        lax.fori_loop(0, 8, step, 0, unroll=4)

    def col(row):
        return jnp.transpose(jnp.broadcast_to(row, (128, 128)))

    ssq[...] = jnp.zeros_like(ssq)
    ssq_block(xl, t)

    def tokens():
        got(tw.at[1 - xl], tw_r)
        tsum[...] = jnp.zeros_like(tsum)
        tsum[0:2, :] = tw[0, 2:4, :] + tw[1, 2:4, :]
        for j in range(3):
            send(tsum, tot_y.at[j], ty_s.at[j], ty_r.at[j], at_y(DY[j]))
        for a in range(2):
            for k in range(2):
                tgtb[a, k * 128:(k + 1) * 128, :] = col(tw[a, k:k + 1, :])
                wb[a, k * 128:(k + 1) * 128, :] = col(tw[a, 2 + k:3 + k, :])

    def t_hop(src, s, d):
        send(src, tot_z.at[s, d], tz_s.at[s, d], tz_r.at[s, d], at_z(SZ[s]))

    def do_ty():
        for j in range(3):
            got(tot_y.at[j], ty_r.at[j])
        tsum2[...] = tsum[...] + tot_y[0] + tot_y[1] + tot_y[2]
        for s in range(2):
            t_hop(tsum2, s, 0)

    def do_tz(d):
        for s in range(2):
            if d <= ring_limit(s):
                got(tot_z.at[s, d - 1], tz_r.at[s, d - 1])
                if d < ring_limit(s):
                    t_hop(tot_z.at[s, d - 1], s, d)

    def do_xe():
        got(hb.at[z, y, 1 - xl], xh_r)
        a_hop(0, 0)
        a_hop(1, 0)
        b_out(2)
        a_out(0)

    def do_by(k):
        got(hb.at[z, ywas(k - 1), xl], by_r.at[k - 1])
        for s in range(2):
            b_hop(s, 0, k)

    def do_az(s, d):
        got(hb.at[zz(-SZ[s] * d), y, 1 - xl], az_r.at[s, d - 1])
        if d < limit(s, -1):
            a_hop(s, d)
        a_out((-SZ[s] * d) % 8)

    def do_bz(s, d, k):
        yk = y if k == 0 else ywas(k - 1)
        got(hb.at[zz(-SZ[s] * d), yk, xl], bz_r.at[s, d - 1, k])
        if d < limit(s, k):
            b_hop(s, d, k)

    def rows_of(i):
        return slice(i * 128, (i + 1) * 128)

    XD = (1, 3, 2)

    def xblock(i):
        xs = (x - XD[i] + 4) % 4
        return xs % 2, (xs // 2) * 2

    def do_xf(i):
        a, b = xblock(i)
        ref = xg.at[a, b + c]
        if i < 2:
            got(ref, hx_r.at[i])
            part = xg.at[a, b + c, rows_of(i)]
            send(part, part, hh_s.at[i], hh_r.at[i], at_x((1, 3)[i]))
        else:
            for h in range(2):
                got(xg.at[a, b + c, rows_of(h)], hh_r.at[h])
        send(ref, ref, hf_s.at[i], hf_r.at[i], at_x(0, 1))
        ssq_block(a, b + c)

    def do_xs(i):
        a, b = xblock(i)
        got(xg.at[a, b + 1 - c], hf_r.at[i])
        ssq_block(a, b + 1 - c)

    def do_xo():
        got(xg.at[xl, xh * 2 + 1 - c], hx_r.at[3])
        ssq_block(xl, xh * 2 + 1 - c)
        for i, (dx, dc) in enumerate(GP):
            ts = ((xh + (dx // 2)) % 2) * 2 + (c + dc) % 2
            got(gg4.at[ts], gn_r.at[i])

    def half(h):
        return (xl + h) % 2

    def do_iv(h):
        a = half(h)
        s_ = jnp.sum(ssq[a], axis=1, keepdims=True)
        invb[a] = jnp.broadcast_to(lax.rsqrt(s_ * (1.0 / D) + EPS), (256, 128))

    def do_nm(h, zb):
        a = half(h)
        t0 = zb // 4
        off = (zb % 4) * 256

        def step(i, carry):
            rows = pl.ds(pl.multiple_of(i * 32, 32), 32)
            out = pl.ds(pl.multiple_of(a * 256 + i * 32, 32), 32)
            inv = invb[a, rows, :]
            low = lax.broadcasted_iota(jnp.int32, (32, 128), 1) < 64
            for p in range(2):
                cols = slice(off + p * 128, off + (p + 1) * 128)
                u = xg[a, t0, rows, cols].astype(F32) * inv * gg4[t0, :, cols]
                v = xg[a, t0 + 2, rows, cols].astype(F32) * inv * gg4[t0 + 2, :, cols]
                ur = pltpu.roll(u, 64, 1)
                vr = pltpu.roll(v, 64, 1)
                nm[zb, out, (2 * p) * 128:(2 * p + 1) * 128] = jnp.where(low, u, vr).astype(BF16)
                nm[zb, out, (2 * p + 1) * 128:(2 * p + 2) * 128] = jnp.where(low, ur, v).astype(BF16)
            return carry
        lax.fori_loop(0, 8, step, 0, unroll=4)

    def do_lg(k):
        for j in range(3):
            got(hb.at[zz(k), ywas(j), 1 - xl], ay_r.at[k, j])
        part = jnp.dot(nm[zz(k)], hb[zz(k)].reshape(512, 512), preferred_element_type=F32)
        if k == 0:
            lg[...] = part
        else:
            lg[...] += part

    steps = dict(
        xe=do_xe, by=do_by, az=do_az, bz=do_bz, xf=do_xf, xs=do_xs, xo=do_xo,
        iv=do_iv, nm=do_nm, lg=do_lg, ty=do_ty, tz=do_tz,
    )
    tokens_done = False
    for name, *arg in GATHER:
        steps[name](*arg)
        if name == "by" and not tokens_done:
            tokens_done = True
            tokens()

    col0 = (t * 1024 + xl * 512).astype(F32)
    me = x * 2 + c

    def stat_step(i, carry):
        rows = pl.ds(pl.multiple_of(i * 32, 32), 32)
        l = lg[rows, :]
        m = jnp.max(l, axis=1, keepdims=True)
        ev = jnp.exp(l - m)
        ex[rows, :] = ev
        e = jnp.sum(ev, axis=1, keepdims=True)
        a = i // 8
        tb = tgtb[a, pl.ds(pl.multiple_of((i % 8) * 32, 32), 32), :][:, 0:1] - col0
        cols = lax.broadcasted_iota(jnp.int32, (32, 512), 1).astype(F32)
        pk = jnp.sum(jnp.where(cols == tb, l, 0.0), axis=1, keepdims=True)
        lane = lax.broadcasted_iota(jnp.int32, (32, 128), 1)
        stat[rows, :] = jnp.where(lane == 0, m, jnp.where(lane == 1, e, jnp.where(lane == 2, pk, 0.0)))
        return carry

    lax.fori_loop(0, 16, stat_step, 0, unroll=4)
    for k in range(4):
        st[me, k] = jnp.transpose(stat[k * 128:(k + 1) * 128, :])[0:8, :]
    for i, (dx, dc) in enumerate(PEERS):
        send(st.at[me], st.at[me], st_s.at[i], st_r.at[i], at_x(dx, dc))

    def peer_was(i):
        dx, dc = PEERS[i]
        return ((x - dx + 4) % 4) * 2 + (c + dc) % 2

    for i in range(7):
        got(st.at[peer_was(i)], st_r.at[i])
    allst = st[...]
    mx = jnp.max(allst[:, :, 0:1, :], axis=0)
    es = jnp.sum(allst[:, :, 1:2, :] * jnp.exp(allst[:, :, 0:1, :] - mx[None]), axis=0)
    pk = jnp.sum(allst[:, :, 2:3, :], axis=0)
    lse = mx + jnp.log(es)
    loss_row = jnp.zeros((1, 128), F32)
    for k in range(4):
        loss_row = loss_row + tw[k // 2, 2 + k % 2:3 + k % 2, :] * (lse[k] - pk[k])
        lseb[k * 128:(k + 1) * 128, :] = col(lse[k])

    def dl_step(i, carry):
        a = i // 8
        rows = pl.ds(pl.multiple_of((i % 8) * 32, 32), 32)
        g = pl.ds(pl.multiple_of(i * 32, 32), 32)
        l = lg[g, :]
        tb = tgtb[a, rows, :][:, 0:1] - col0
        w = wb[a, rows, :][:, 0:1]
        cols = lax.broadcasted_iota(jnp.int32, (32, 512), 1).astype(F32)
        p = ex[g, :] * jnp.exp(stat[g, :][:, 0:1] - lseb[g, :][:, 0:1])
        d = (w * (p - jnp.where(cols == tb, 1.0, 0.0))).astype(BF16)
        dl[a, rows, :] = d
        q = jnp.sum(d.astype(F32) * l, axis=1, keepdims=True)
        stat[g, :] = jnp.broadcast_to(q, (32, 128))
        return carry

    lax.fori_loop(0, 16, dl_step, 0, unroll=4)
    for a in range(2):
        dlt[:, a * 256:(a + 1) * 256] = jnp.transpose(dl[a])

    for k in range(4):
        qt[me, k] = jnp.transpose(stat[k * 128:(k + 1) * 128, :])[0:8, :]
    for i, (dx, dc) in enumerate(PEERS):
        send(qt.at[me], qt.at[me], qt_s.at[i], qt_r.at[i], at_x(dx, dc))

    def do_hg(k):
        g = jnp.dot(dlt[...], nm[zz(k)], preferred_element_type=F32)
        for b in range(4):
            ght[k, b] = g[:, b * 128:(b + 1) * 128]
        for j in range(3):
            sba[k, j] = ght[k, yy(DY[j]), 0:256, :].astype(BF16)
            send(sba.at[k, j], rba.at[k, j], ra_s.at[k, j], ra_r.at[k, j], at_y(DY[j]))

    def qrows(q):
        return slice(256 + q * 64, 320 + q * 64)

    def do_bc(s, d, q):
        k = (SZ[s] * d) % 8
        v = ght[k, :, qrows(q), :]
        if d < (4 if q % 2 == s else 3):
            got(rbb.at[s, q, d], rb_r.at[s, q, d])
            v = v + rbb[s, q, d].astype(F32)
        sbb[s, q, d - 1] = v.astype(BF16)
        send(sbb.at[s, q, d - 1], rbb.at[s, q, d - 1], rb_s.at[s, q, d - 1], rb_r.at[s, q, d - 1], at_z(SZ[s]))

    def a_sum(k):
        v = ght[k, y, 0:256, :]
        for j in range(3):
            got(rba.at[k, j], ra_r.at[k, j])
            v = v + rba[k, j].astype(F32)
        return v

    def do_a4():
        fa[...] = a_sum(4)
        for s in range(2):
            h = slice(s * 128, (s + 1) * 128)
            sa4[s] = fa[h, :].astype(BF16)
            send(sa4.at[s], ra4.at[s], rz_s.at[s, 3], rz_r.at[s, 3], at_z(SZ[s]))

    def do_ac(s, d):
        v = a_sum((SZ[s] * d) % 8)
        if d == 3:
            h = slice(s * 128, (s + 1) * 128)
            sa3[s] = v.astype(BF16)
            got(ra4.at[s], rz_r.at[s, 3])
            sa3[s, h] = (v[h] + ra4[s].astype(F32)).astype(BF16)
            send(sa3.at[s], ra3.at[s], rz_s.at[s, 2], rz_r.at[s, 2], at_z(SZ[s]))
            return
        if d == 2:
            got(ra3.at[s], rz_r.at[s, 2])
            sa2[s, 1] = v + ra3[s].astype(F32)
        else:
            got(ra2.at[s, 1], rz_r.at[s, 1])
            sa2[s, 0] = v + ra2[s, 1]
        send(sa2.at[s, d - 1], ra2.at[s, d - 1], rz_s.at[s, d - 1], rz_r.at[s, d - 1], at_z(SZ[s]))

    XO = (2, 1, 3, 0)

    def xdest(n):
        xs = (x + XO[n]) % 4
        return xs % 2, xs // 2

    def dn_part(out, n, cc):
        a, b = xdest(n)
        for i in range(4):
            h = hb[4 * cc + i, :, b].reshape(256, 512)
            out[n, :, i * 256:(i + 1) * 256] = lax.dot_general(
                dl[a], h, (((1,), (1,)), ((), ())), preferred_element_type=F32
            )

    def do_ds(n):
        dn_part(dns, n, 1 - c)
        send(dns.at[n], dnr.at[n], dc_s.at[n], dc_r.at[n], at_x(0, 1))
        dn_part(dno, n, c)

    def x_out(i):
        src = dno.at[1 + i, rows_of(i)]
        send(src, rbx.at[i], dx_s.at[i], dx_r.at[i], at_x((1, 3)[i]))

    def x_one(i):
        dos[i] = dno[1 + i, rows_of(1 - i), :].astype(BF16)
        send(dos.at[i], dor.at[1 - i], do_s.at[i], do_r.at[i], at_x((1, 3)[i]))

    def do_du(n):
        got(dnr.at[n], dc_r.at[n])
        a, b = xdest(n)
        tx = b * 2 + c

        def step(i, acc):
            rows = pl.ds(pl.multiple_of(i * 16, 16), 16)
            s_ = dno[n, rows, :] + dnr[n, rows, :]
            if n == 0:
                dxs[rows, :] = s_.astype(BF16)
            else:
                dno[n, rows, :] = s_
            xv = xg[a, tx, rows, :].astype(F32) * invb[a, rows, :][:, 0:1]
            pr = s_ * xv
            return acc + pr[0:8] + pr[8:16]
        acc = lax.fori_loop(0, 16, step, jnp.zeros((8, 1024), F32), unroll=2)
        gps[b * 2 + a] = jnp.sum(acc, axis=0, keepdims=True)
        if n == 0:
            for i in range(2):
                send(dxs.at[rows_of(i)], dxr.at[i], d2_s.at[i], d2_r.at[i], at_x((1, 3)[i]))
        elif n == 1:
            x_one(0)
        elif n == 2:
            x_one(1)

    def do_xr(n):
        i = n - 1
        got(dxr.at[i], d2_r.at[i])
        dno[n, rows_of(i), :] = dno[n, rows_of(i), :] + dxr[i].astype(F32)
        x_out(i)

    results = []

    def result(src, dst, i):
        cp = pltpu.make_async_copy(src, dst, out_s.at[i])
        cp.start()
        results.append(cp)

    def do_gy():
        for b in range(2):
            msg[b] = gps[2 * b] + gps[2 * b + 1]
        msg[2] = jnp.zeros((1, 1024), F32)
        msg[2, :, 0:128] = loss_row
        for j in range(3):
            send(msg, ary.at[j], gy_s.at[j], gy_r.at[j], at_y(DY[j]))

    def do_gz():
        for j in range(3):
            got(ary.at[j], gy_r.at[j])
        ary[3] = msg[...] + ary[0] + ary[1] + ary[2]
        for d in range(1, 8):
            send(ary.at[3], arz.at[d - 1], gz_s.at[d - 1], gz_r.at[d - 1], at_z(d))

    def do_gx():
        g = ary[3]
        for d in range(7):
            got(arz.at[d], gz_r.at[d])
            g = g + arz[d]
        gxs[...] = g
        for i, dx in enumerate((1, 3, 2)):
            b = ((x + dx) % 4) // 2
            send(gxs.at[b], gxr.at[i], gx_s.at[i], gx_r.at[i], at_x(dx))

    def total_inverse():
        tot = tsum2[...]
        for s in range(2):
            for d in range(ring_limit(s)):
                tot = tot + tot_z[s, d]
        return 1.0 / jnp.sum(jnp.sum(tot, axis=1, keepdims=True), axis=0, keepdims=True)

    def do_gf():
        for i in range(3):
            got(gxr.at[i], gx_r.at[i])
        o_gg[...] = (gxs[xh] + gxr[0] + gxr[1] + gxr[2]) * inv_total
        o_loss[...] = jnp.sum(gxs[2], axis=1, keepdims=True) * inv_total
        result(o_loss, r_loss, 0)
        result(o_gg, r_gg, 1)

    def do_qt():
        for i in range(7):
            got(qt.at[peer_was(i)], qt_r.at[i])
        qsum = qt[0]
        for i in range(1, 8):
            qsum = qsum + qt[i]
        for k in range(4):
            lseb[k * 128:(k + 1) * 128, :] = col(qsum[k, 0:1, :])

    PARTS = (slice(0, 256), slice(256, 384), slice(384, 512))

    def turn(i, v):
        ft = jnp.transpose(v)
        for a in range(2):
            ghs[a, :, PARTS[i]] = ft[a * 64:(a + 1) * 64]
        send(ghs.at[1 - xl, :, PARTS[i]], ghr.at[:, PARTS[i]], fx_s.at[i], fx_r.at[i], mate)

    def do_af():
        va = a_sum(0)
        for s in range(2):
            got(ra2.at[s, 0], rz_r.at[s, 0])
            va = va + ra2[s, 0]
        fa[...] = va
        turn(0, fa[...])

    def do_bf(q):
        v = ght[0, :, qrows(q), :]
        for s in range(2):
            got(rbb.at[s, q, 0], rb_r.at[s, q, 0])
            v = v + rbb[s, q, 0].astype(F32)
        syb[q] = v
        for j in range(3):
            src = syb.at[q, yy(DY[j])]
            send(src, ryb.at[q, j], ry_s.at[q, j], ry_r.at[q, j], at_y(DY[j]))

    def do_bg(p):
        for h in range(2):
            q = 2 * p + h
            v = syb[q, y]
            for j in range(3):
                got(ryb.at[q, j], ry_r.at[q, j])
                v = v + ryb[q, j]
            fb[p, h * 64:(h + 1) * 64, :] = v
        turn(1 + p, fb[p])

    def do_gh():
        o_gh[:, pl.ds(own, 512)] = ghs[xl] * inv_total
        for i in range(3):
            got(ghr.at[:, PARTS[i]], fx_r.at[i])
        o_gh[:, pl.ds(oth, 512)] = ghr[...] * inv_total
        result(o_gh, r_gh, 2)

    def do_fi():
        for i in range(2):
            got(rbx.at[i], dx_r.at[i])
            got(dor.at[1 - i], do_r.at[i])
        gt = gg4[t]

        def fin(i, carry):
            rows = pl.ds(pl.multiple_of(i * 16, 16), 16)
            qrow = pl.ds(pl.multiple_of(xl * 256 + i * 16, 16), 16)
            h = i // 8
            half_rows = pl.ds(pl.multiple_of((i % 8) * 16, 16), 16)
            dn = dno[3, rows, :] + rbx[h, half_rows, :] + dor[h, half_rows, :].astype(F32)
            inv = invb[xl, rows, :][:, 0:1]
            q = lseb[qrow, :][:, 0:1]
            xv = xg[xl, t, rows, :].astype(F32)
            u = inv * inv_total
            o_hid[rows, :] = (dn * gt * u - xv * (inv * u * q * (1.0 / D))).astype(BF16)
            return carry

        lax.fori_loop(0, 16, fin, 0, unroll=2)
        result(o_hid, r_hid, 3)

    steps = dict(
        ds=do_ds, hg=do_hg, bc=do_bc, du=do_du, a4=do_a4, ac=do_ac, xr=do_xr, gy=do_gy, gz=do_gz,
        gx=do_gx, gf=do_gf, qt=do_qt, tz=do_tz, af=do_af, bf=do_bf, bg=do_bg, gh=do_gh, fi=do_fi,
    )
    for name, *arg in SCATTER:
        steps[name](*arg)
        if name == "tz" and arg[0] == 4:
            inv_total = total_inverse()
    for cp in sent:
        cp.wait_send()
    for cp in results:
        cp.wait()


def finish(*refs):
    ins, outs, bufs, sem_in, sem_out = refs[0:4], refs[4:8], refs[8:12], refs[12], refs[13]
    first = [pltpu.make_async_copy(ins[i], bufs[i], sem_in.at[i]) for i in range(4)]
    second = [pltpu.make_async_copy(bufs[i], outs[i], sem_out.at[i]) for i in range(4)]
    for cp in first:
        cp.start()
    for one, two in zip(first, second):
        one.wait()
        two.start()
    for cp in second:
        cp.wait()


def body(hidden, gain, head, targets, row_weight):
    V = pltpu.VMEM
    S = pltpu.SemaphoreType.DMA
    hbm = pl.BlockSpec(memory_space=pl.ANY)
    scratch = [
        V((2, 128), jnp.int32),
        V((2, 128), jnp.int32),
        V((1, 1), F32),
        V((64, 1024), F32),
        V((1, 1024), F32),
        V((256, 1024), BF16),
        V((64, 1024), BF16),
        V((8, 4, 2, 64, 512), BF16),
        V((2, 4, 256, 1024), BF16),
        V((8, 512, 512), BF16),
        V((4, 1, 1024), F32),
        V((2, 8, 128), F32),
        V((2, 256, 128), F32),
        V((2, 256, 128), F32),
        V((2, 256, 128), F32),
        V((2, 256, 128), F32),
        V((512, 512), F32),
        V((512, 512), F32),
        V((2, 256, 512), BF16),
        V((512, 512), BF16),
        V((8, 4, 8, 128), F32),
        V((8, 4, 8, 128), F32),
        V((512, 128), F32),
        V((512, 128), F32),
        V((8, 4, 512, 128), F32),
        V((8, 3, 256, 128), BF16),
        V((8, 3, 256, 128), BF16),
        V((2, 128, 128), BF16),
        V((2, 128, 128), BF16),
        V((2, 256, 128), BF16),
        V((2, 256, 128), BF16),
        V((2, 2, 256, 128), F32),
        V((2, 2, 256, 128), F32),
        V((2, 4, 4, 4, 64, 128), BF16),
        V((2, 4, 4, 4, 64, 128), BF16),
        V((4, 4, 64, 128), F32),
        V((4, 3, 64, 128), F32),
        V((256, 128), F32),
        V((2, 128, 128), F32),
        V((2, 64, 512), F32),
        V((64, 512), F32),
        V((4, 256, 1024), F32),
        V((4, 256, 1024), F32),
        V((4, 256, 1024), F32),
        V((256, 1024), BF16),
        V((2, 128, 1024), BF16),
        V((2, 128, 1024), BF16),
        V((2, 128, 1024), BF16),
        V((2, 128, 1024), F32),
        V((4, 1, 1024), F32),
        V((3, 1, 1024), F32),
        V((3, 1, 1024), F32),
        V((3, 1, 1024), F32),
        V((4, 3, 1, 1024), F32),
        V((7, 3, 1, 1024), F32),
        V((8, 128), F32),
        V((8, 128), F32),
        V((3, 8, 128), F32),
        V((2, 4, 8, 128), F32),
        S((5,)),
        S((4,)),
    ]
    shapes = [
        (), (), (3,), (4,), (2,), (3,),
        (2, 4), (8, 3), (3,), (2, 4, 4),
        (7,), (7,), (3,), (2, 4),
        (8, 3), (2, 4), (2, 4, 4), (4, 3), (3,),
        (4,), (2,), (2,), (2,), (3,), (3,), (7,),
    ]
    for sh in shapes:
        scratch += [S(sh), S(sh)] if sh else [S, S]
    loss, gh, gg, gx = pl.pallas_call(
        kernel,
        out_shape=(
            jax.ShapeDtypeStruct((1, 1), F32),
            jax.ShapeDtypeStruct((64, 1024), F32),
            jax.ShapeDtypeStruct((1, 1024), F32),
            jax.ShapeDtypeStruct((256, 1024), BF16),
        ),
        in_specs=[hbm] * 5,
        out_specs=(hbm,) * 4,
        scratch_shapes=scratch,
        compiler_params=pltpu.CompilerParams(
            collective_id=0, has_side_effects=True, vmem_limit_bytes=62 << 20
        ),
    )(hidden, gain.reshape(1, 1024), head, targets.reshape(2, 128), row_weight.reshape(2, 128))
    loss, gh, gg, gx = pl.pallas_call(
        finish,
        out_shape=tuple(jax.ShapeDtypeStruct(a.shape, a.dtype) for a in (loss, gh, gg, gx)),
        in_specs=[hbm] * 4,
        out_specs=(hbm,) * 4,
        scratch_shapes=[V(a.shape, a.dtype) for a in (loss, gh, gg, gx)] + [S((4,)), S((4,))],
        compiler_params=pltpu.CompilerParams(vmem_limit_bytes=62 << 20),
    )(loss, gh, gg, gx)
    return (loss.reshape(()), gh, gg.reshape(1024), gx)


def solution(mesh):
    in_specs = (P("fsdp", "tp"), P("tp"), P("fsdp", "tp"), P("fsdp"), P("fsdp"))
    out_specs = (P(), P("fsdp", "tp"), P("tp"), P("fsdp", "tp"))
    return jax.shard_map(body, mesh=mesh, in_specs=in_specs, out_specs=out_specs, check_vma=False)
```

time: 141 us -> 94.5 us (0.67)
  Pallas kernels: 136 us -> 93.7 us
  local copies, waits for them, and re-layouts: 4.31 us -> 0 us
    pallas_call x1 -> x2, Pallas kernels: 136 us -> 93.7 us  [the longest x1 91.1 us: body(): pl.pallas_call(kernel, out_shape=(jax.ShapeDtypeStruct((1, 1), F32), jax....]
    unnamed x7 -> x0, local copies, waits for them, and re-layouts: 3.07 us -> none
where the time goes in v2:
time: 94.5 us; the launch traced here: 94.4 us
  Pallas kernels  93.7 us (99%)
    pallas_call x1, Pallas kernels, body(): pl.pallas_call(kernel, out_shape=(jax.ShapeDtypeStruct((1, 1), F32), jax....  91.1 us
    pallas_call x1, Pallas kernels, body(): pl.pallas_call(finish, out_shape=tuple((jax.ShapeDtypeStruct(a.shape, a.d...  2.62 us

profile of v2, /device:TPU:2, one launch (start us, length us, event | category | flops | bytes accessed | tf_op | source)
XLA Modules:
  0.0 94.4 jit_solution(3025669825867226872)
XLA Ops:
  0.6 91.1 %shard_map.84 = (f32[1,1]{1,0:T(1,128)}, f32[64,1024]{1,0:T(8,128)}, f32[1,1024]{1,0:T(1,128)}, bf16[256,1024]{1,0:T(8,128)(2,1)}) custom-call(bf16[256,1024]{1,0:T(8,128)(2,1)} %hid.1, f32[1,1024]{1,0:T(1,128)} %bitcast.5, bf16[64,1024]{1,0:T(8,128)(2,1)} %hin_hbm.1, s32[2,128]{1,0:T(2,128)} %bitcast.6, s32[2,128]{1,0:T(2,128)} %bitcast.7), custom_call_target="tpu_custom_call" | custom-call | tf_op jit(solution)/shard_map/pallas_call | solution.py:718
  91.8 2.6 %shard_map.85 = (f32[1,1]{1,0:T(1,128)}, f32[64,1024]{1,0:T(8,128)}, f32[1,1024]{1,0:T(1,128)}, bf16[256,1024]{1,0:T(8,128)(2,1)}) custom-call(f32[1,1]{1,0:T(1,128)} %get-tuple-element.12.refs_0_, f32[64,1024]{1,0:T(8,128)} %get-tuple-element.13.refs_1_, f32[1,1024]{1,0:T(1,128)} %get-tuple-element.14.refs_2_, bf16[256,1024]{1,0:T(8,128)(2,1)} %get-tuple-element.15.refs_3_), custom_call_target="tpu_custom_call" | custom-call | tf_op jit(solution)/shard_map/pallas_call | solution.py:733

commit v3 on v2

--- a/solution.py
+++ b/solution.py
@@ -32,12 +32,12 @@
     ("hg", 4), ("bc", 0, 4, 0), ("bc", 1, 4, 1), ("bc", 0, 4, 2), ("bc", 1, 4, 3), ("hg", 3), ("bc", 0, 3, 1),
     ("bc", 0, 3, 3), ("hg", 5), ("bc", 1, 3, 0), ("bc", 1, 3, 2), ("ds", 0), ("hg", 2), ("ds", 1), ("du", 0),
     ("bc", 0, 3, 0), ("bc", 1, 3, 1), ("ds", 2), ("bc", 0, 3, 2), ("bc", 1, 3, 3), ("hg", 6), ("a4",), ("du", 1),
-    ("bc", 0, 2, 1), ("bc", 1, 2, 0), ("ds", 3), ("du", 2), ("bc", 0, 2, 3), ("bc", 1, 2, 2), ("du", 3), ("gy",),
+    ("bc", 0, 2, 1), ("bc", 1, 2, 0), ("ds", 3), ("du", 2), ("bc", 0, 2, 3), ("bc", 1, 2, 2), ("du", 3), ("gx",),
     ("hg", 1), ("bc", 0, 2, 0), ("bc", 1, 2, 1), ("hg", 7), ("hg", 0), ("xr", 1), ("xr", 2), ("ac", 0, 3),
     ("ac", 1, 3), ("bc", 0, 2, 2), ("bc", 1, 2, 3), ("bc", 0, 1, 1), ("bc", 1, 1, 0), ("tz", 3), ("bc", 0, 1, 3),
-    ("bc", 1, 1, 2), ("bc", 0, 1, 0), ("bc", 1, 1, 1), ("ac", 0, 2), ("ac", 1, 2), ("gz",), ("bc", 0, 1, 2),
-    ("bc", 1, 1, 3), ("tz", 4), ("qt",), ("bf", 0), ("bf", 1), ("ac", 0, 1), ("ac", 1, 1), ("bf", 2), ("bf", 3),
-    ("gx",), ("bg", 0), ("bg", 1), ("af",), ("fi",), ("gf",), ("gh",),
+    ("bc", 1, 1, 2), ("bc", 0, 1, 0), ("bc", 1, 1, 1), ("bc", 0, 1, 2), ("bc", 1, 1, 3), ("ac", 0, 2),
+    ("ac", 1, 2), ("gy",), ("tz", 4), ("qt",), ("bf", 0), ("bf", 1), ("ac", 0, 1), ("ac", 1, 1), ("gz",), ("bf", 2),
+    ("bf", 3), ("bg", 0), ("bg", 1), ("af",), ("fi",), ("gf",), ("gh",),
 )
 
 
@@ -48,12 +48,9 @@
     st, qt, lseb, stat,
     ght, sba, rba, sa4, ra4, sa3, ra3, sa2, ra2, sbb, rbb, syb, ryb, fa, fb, ghs, ghr,
     dno, dns, dnr, dxs, dxr, dos, dor, rbx, gps, gxs, gxr, msg, ary, arz, tsum, tsum2, tot_y, tot_z,
-    in_s, out_s,
-    xh_s, xh_r, tw_s, tw_r, gn_s, gn_r, hx_s, hx_r, hh_s, hh_r, hf_s, hf_r,
-    az_s, az_r, ay_s, ay_r, by_s, by_r, bz_s, bz_r,
-    st_s, st_r, qt_s, qt_r, ty_s, ty_r, tz_s, tz_r,
-    ra_s, ra_r, rz_s, rz_r, rb_s, rb_r, ry_s, ry_r, fx_s, fx_r,
-    dc_s, dc_r, d2_s, d2_r, dx_s, dx_r, do_s, do_r, gx_s, gx_r, gy_s, gy_r, gz_s, gz_r,
+    in_s, out_s, send_s,
+    xh_r, tw_r, gn_r, hx_r, hh_r, hf_r, az_r, ay_r, by_r, bz_r, st_r, qt_r, ty_r, tz_r,
+    ra_r, rz_r, rb_r, ry_r, fx_r, dc_r, d2_r, dx_r, do_r, gx_r, gy_r, gz_r,
 ):
     f = lax.axis_index("fsdp")
     t = lax.axis_index("tp")
@@ -104,17 +101,20 @@
     hb[z, y, xl] = hin[:, pl.ds(own, 512)]
     pl.semaphore_wait(barrier, len(partners))
 
-    sent = []
+    sent = [0, 0, 0]
+    GATHER_S, SEND_S, X_S = range(3)
 
     def rc(src, dst, ss, rs, to):
         return pltpu.make_async_remote_copy(
             src_ref=src, dst_ref=dst, send_sem=ss, recv_sem=rs, device_id=to, device_id_type=MESH
         )
 
-    def send(src, dst, ss, rs, to):
-        cp = rc(src, dst, ss, rs, to)
-        cp.start()
-        sent.append(cp)
+    def send(src, dst, group, rs, to):
+        rc(src, dst, send_s.at[group], rs, to).start()
+        size = jnp.dtype(src.dtype).itemsize
+        for n in src.shape:
+            size *= n
+        sent[group] += size
 
     def got(dst, rs):
         rc(dst, dst, rs, rs, at_y(1)).wait_recv()
@@ -122,16 +122,16 @@
     def b_hop(s, d, k):
         yk = y if k == 0 else ywas(k - 1)
         ref = hb.at[zz(-SZ[s] * d), yk, xl]
-        send(ref, ref, bz_s.at[s, d, k], bz_r.at[s, d, k], at_z(SZ[s]))
+        send(ref, ref, GATHER_S, bz_r.at[s, d, k], at_z(SZ[s]))
 
     def a_hop(s, d):
         ref = hb.at[zz(-SZ[s] * d), y, 1 - xl]
-        send(ref, ref, az_s.at[s, d], az_r.at[s, d], at_z(SZ[s]))
+        send(ref, ref, GATHER_S, az_r.at[s, d], at_z(SZ[s]))
 
     def a_out(k):
         ref = hb.at[zz(k), y, 1 - xl]
         for j in range(3):
-            send(ref, ref, ay_s.at[k, j], ay_r.at[k, j], at_y(DY[j]))
+            send(ref, ref, GATHER_S, ay_r.at[k], at_y(DY[j]))
 
     def ywas(j):
         return yy(-DY[j])
@@ -144,10 +144,10 @@
     def ring_limit(s):
         return 4 if s == 0 else 3
 
-    send(hin.at[:, pl.ds(oth, 512)], hb.at[z, y, xl], xh_s, xh_r, mate)
+    send(hin.at[:, pl.ds(oth, 512)], hb.at[z, y, xl], GATHER_S, xh_r, mate)
     def b_out(j):
         ref = hb.at[z, y, xl]
-        send(ref, ref, by_s.at[j], by_r.at[j], at_y(DY[j]))
+        send(ref, ref, GATHER_S, by_r.at[j], at_y(DY[j]))
 
     b_out(0)
     b_out(1)
@@ -157,13 +157,13 @@
         cp.wait()
     tw[xl, 0:2, :] = tgt[...].astype(F32)
     tw[xl, 2:4, :] = wgt[...].astype(F32)
-    send(tw.at[xl], tw.at[xl], tw_s, tw_r, mate)
+    send(tw.at[xl], tw.at[xl], GATHER_S, tw_r, mate)
     GP = ((0, 1), (2, 0), (2, 1))
     for i, (dx, dc) in enumerate(GP):
-        send(gg4.at[t], gg4.at[t], gn_s.at[i], gn_r.at[i], at_x(dx, dc))
+        send(gg4.at[t], gg4.at[t], GATHER_S, gn_r, at_x(dx, dc))
     in_hid.wait()
     for i, dx, dc in ((3, 0, 1), (0, 1, 0), (1, 3, 0)):
-        send(xg.at[xl, t], xg.at[xl, t], hx_s.at[i], hx_r.at[i], at_x(dx, dc))
+        send(xg.at[xl, t], xg.at[xl, t], GATHER_S, hx_r.at[i], at_x(dx, dc))
 
     def ssq_block(xl_, t_):
         def step(i, carry):
@@ -188,18 +188,17 @@
         tsum[...] = jnp.zeros_like(tsum)
         tsum[0:2, :] = tw[0, 2:4, :] + tw[1, 2:4, :]
         for j in range(3):
-            send(tsum, tot_y.at[j], ty_s.at[j], ty_r.at[j], at_y(DY[j]))
+            send(tsum, tot_y.at[j], SEND_S, ty_r, at_y(DY[j]))
         for a in range(2):
             for k in range(2):
                 tgtb[a, k * 128:(k + 1) * 128, :] = col(tw[a, k:k + 1, :])
                 wb[a, k * 128:(k + 1) * 128, :] = col(tw[a, 2 + k:3 + k, :])
 
     def t_hop(src, s, d):
-        send(src, tot_z.at[s, d], tz_s.at[s, d], tz_r.at[s, d], at_z(SZ[s]))
+        send(src, tot_z.at[s, d], SEND_S, tz_r.at[s, d], at_z(SZ[s]))
 
     def do_ty():
-        for j in range(3):
-            got(tot_y.at[j], ty_r.at[j])
+        got(tot_y, ty_r)
         tsum2[...] = tsum[...] + tot_y[0] + tot_y[1] + tot_y[2]
         for s in range(2):
             t_hop(tsum2, s, 0)
@@ -250,11 +249,11 @@
         if i < 2:
             got(ref, hx_r.at[i])
             part = xg.at[a, b + c, rows_of(i)]
-            send(part, part, hh_s.at[i], hh_r.at[i], at_x((1, 3)[i]))
+            send(part, part, GATHER_S, hh_r.at[i], at_x((1, 3)[i]))
         else:
             for h in range(2):
                 got(xg.at[a, b + c, rows_of(h)], hh_r.at[h])
-        send(ref, ref, hf_s.at[i], hf_r.at[i], at_x(0, 1))
+        send(ref, ref, GATHER_S, hf_r.at[i], at_x(0, 1))
         ssq_block(a, b + c)
 
     def do_xs(i):
@@ -265,9 +264,7 @@
     def do_xo():
         got(xg.at[xl, xh * 2 + 1 - c], hx_r.at[3])
         ssq_block(xl, xh * 2 + 1 - c)
-        for i, (dx, dc) in enumerate(GP):
-            ts = ((xh + (dx // 2)) % 2) * 2 + (c + dc) % 2
-            got(gg4.at[ts], gn_r.at[i])
+        got(gg4.at[0:3], gn_r)
 
     def half(h):
         return (xl + h) % 2
@@ -299,8 +296,7 @@
         lax.fori_loop(0, 8, step, 0, unroll=4)
 
     def do_lg(k):
-        for j in range(3):
-            got(hb.at[zz(k), ywas(j), 1 - xl], ay_r.at[k, j])
+        got(hb.at[0:3, 0, 0], ay_r.at[k])
         part = jnp.dot(nm[zz(k)], hb[zz(k)].reshape(512, 512), preferred_element_type=F32)
         if k == 0:
             lg[...] = part
@@ -340,14 +336,9 @@
     for k in range(4):
         st[me, k] = jnp.transpose(stat[k * 128:(k + 1) * 128, :])[0:8, :]
     for i, (dx, dc) in enumerate(PEERS):
-        send(st.at[me], st.at[me], st_s.at[i], st_r.at[i], at_x(dx, dc))
-
-    def peer_was(i):
-        dx, dc = PEERS[i]
-        return ((x - dx + 4) % 4) * 2 + (c + dc) % 2
-
-    for i in range(7):
-        got(st.at[peer_was(i)], st_r.at[i])
+        send(st.at[me], st.at[me], SEND_S, st_r, at_x(dx, dc))
+
+    got(st.at[0:7], st_r)
     allst = st[...]
     mx = jnp.max(allst[:, :, 0:1, :], axis=0)
     es = jnp.sum(allst[:, :, 1:2, :] * jnp.exp(allst[:, :, 0:1, :] - mx[None]), axis=0)
@@ -380,32 +371,35 @@
     for k in range(4):
         qt[me, k] = jnp.transpose(stat[k * 128:(k + 1) * 128, :])[0:8, :]
     for i, (dx, dc) in enumerate(PEERS):
-        send(qt.at[me], qt.at[me], qt_s.at[i], qt_r.at[i], at_x(dx, dc))
+        send(qt.at[me], qt.at[me], SEND_S, qt_r, at_x(dx, dc))
+
+    def a_rows(k, b):
+        return pl.ds(pl.multiple_of((k * 4 + b) * 512, 512), 256)
+
+    def b_rows(k, q):
+        return [ght[(k * 4 + b) * 512 + 256 + q * 64:(k * 4 + b) * 512 + 320 + q * 64, :] for b in range(4)]
 
     def do_hg(k):
         g = jnp.dot(dlt[...], nm[zz(k)], preferred_element_type=F32)
         for b in range(4):
-            ght[k, b] = g[:, b * 128:(b + 1) * 128]
+            ght[(k * 4 + b) * 512:(k * 4 + b + 1) * 512, :] = g[:, b * 128:(b + 1) * 128]
         for j in range(3):
-            sba[k, j] = ght[k, yy(DY[j]), 0:256, :].astype(BF16)
-            send(sba.at[k, j], rba.at[k, j], ra_s.at[k, j], ra_r.at[k, j], at_y(DY[j]))
-
-    def qrows(q):
-        return slice(256 + q * 64, 320 + q * 64)
+            sba[k, j] = ght[a_rows(k, yy(DY[j])), :].astype(BF16)
+            send(sba.at[k, j], rba.at[k, j], SEND_S, ra_r.at[k], at_y(DY[j]))
 
     def do_bc(s, d, q):
-        k = (SZ[s] * d) % 8
-        v = ght[k, :, qrows(q), :]
+        v = b_rows((SZ[s] * d) % 8, q)
         if d < (4 if q % 2 == s else 3):
             got(rbb.at[s, q, d], rb_r.at[s, q, d])
-            v = v + rbb[s, q, d].astype(F32)
-        sbb[s, q, d - 1] = v.astype(BF16)
-        send(sbb.at[s, q, d - 1], rbb.at[s, q, d - 1], rb_s.at[s, q, d - 1], rb_r.at[s, q, d - 1], at_z(SZ[s]))
+            v = [v[b] + rbb[s, q, d, b].astype(F32) for b in range(4)]
+        for b in range(4):
+            sbb[s, q, d - 1, b] = v[b].astype(BF16)
+        send(sbb.at[s, q, d - 1], rbb.at[s, q, d - 1], SEND_S, rb_r.at[s, q, d - 1], at_z(SZ[s]))
 
     def a_sum(k):
-        v = ght[k, y, 0:256, :]
+        v = ght[a_rows(k, y), :]
+        got(rba.at[k], ra_r.at[k])
         for j in range(3):
-            got(rba.at[k, j], ra_r.at[k, j])
             v = v + rba[k, j].astype(F32)
         return v
 
@@ -414,7 +408,7 @@
         for s in range(2):
             h = slice(s * 128, (s + 1) * 128)
             sa4[s] = fa[h, :].astype(BF16)
-            send(sa4.at[s], ra4.at[s], rz_s.at[s, 3], rz_r.at[s, 3], at_z(SZ[s]))
+            send(sa4.at[s], ra4.at[s], SEND_S, rz_r.at[s, 3], at_z(SZ[s]))
 
     def do_ac(s, d):
         v = a_sum((SZ[s] * d) % 8)
@@ -423,7 +417,7 @@
             sa3[s] = v.astype(BF16)
             got(ra4.at[s], rz_r.at[s, 3])
             sa3[s, h] = (v[h] + ra4[s].astype(F32)).astype(BF16)
-            send(sa3.at[s], ra3.at[s], rz_s.at[s, 2], rz_r.at[s, 2], at_z(SZ[s]))
+            send(sa3.at[s], ra3.at[s], SEND_S, rz_r.at[s, 2], at_z(SZ[s]))
             return
         if d == 2:
             got(ra3.at[s], rz_r.at[s, 2])
@@ -431,7 +425,7 @@
         else:
             got(ra2.at[s, 1], rz_r.at[s, 1])
             sa2[s, 0] = v + ra2[s, 1]
-        send(sa2.at[s, d - 1], ra2.at[s, d - 1], rz_s.at[s, d - 1], rz_r.at[s, d - 1], at_z(SZ[s]))
+        send(sa2.at[s, d - 1], ra2.at[s, d - 1], SEND_S, rz_r.at[s, d - 1], at_z(SZ[s]))
 
     XO = (2, 1, 3, 0)
 
@@ -449,16 +443,16 @@
 
     def do_ds(n):
         dn_part(dns, n, 1 - c)
-        send(dns.at[n], dnr.at[n], dc_s.at[n], dc_r.at[n], at_x(0, 1))
+        send(dns.at[n], dnr.at[n], X_S, dc_r.at[n], at_x(0, 1))
         dn_part(dno, n, c)
 
     def x_out(i):
         src = dno.at[1 + i, rows_of(i)]
-        send(src, rbx.at[i], dx_s.at[i], dx_r.at[i], at_x((1, 3)[i]))
+        send(src, rbx.at[i], X_S, dx_r.at[i], at_x((1, 3)[i]))
 
     def x_one(i):
         dos[i] = dno[1 + i, rows_of(1 - i), :].astype(BF16)
-        send(dos.at[i], dor.at[1 - i], do_s.at[i], do_r.at[i], at_x((1, 3)[i]))
+        send(dos.at[i], dor.at[1 - i], X_S, do_r.at[i], at_x((1, 3)[i]))
 
     def do_du(n):
         got(dnr.at[n], dc_r.at[n])
@@ -479,7 +473,7 @@
         gps[b * 2 + a] = jnp.sum(acc, axis=0, keepdims=True)
         if n == 0:
             for i in range(2):
-                send(dxs.at[rows_of(i)], dxr.at[i], d2_s.at[i], d2_r.at[i], at_x((1, 3)[i]))
+                send(dxs.at[rows_of(i)], dxr.at[i], X_S, d2_r.at[i], at_x((1, 3)[i]))
         elif n == 1:
             x_one(0)
         elif n == 2:
@@ -498,30 +492,25 @@
         cp.start()
         results.append(cp)
 
+    def do_gx():
+        for b in range(2):
+            gxs[b] = gps[2 * b] + gps[2 * b + 1]
+        for i, dx in enumerate((1, 3, 2)):
+            b = ((x + dx) % 4) // 2
+            send(gxs.at[b], gxr.at[i], SEND_S, gx_r, at_x(dx))
+
     def do_gy():
-        for b in range(2):
-            msg[b] = gps[2 * b] + gps[2 * b + 1]
-        msg[2] = jnp.zeros((1, 1024), F32)
-        msg[2, :, 0:128] = loss_row
+        got(gxr, gx_r)
+        msg[:, 0:1024] = gxs[xh] + gxr[0] + gxr[1] + gxr[2]
+        msg[:, 1024:1152] = loss_row
         for j in range(3):
-            send(msg, ary.at[j], gy_s.at[j], gy_r.at[j], at_y(DY[j]))
+            send(msg, ary.at[j], SEND_S, gy_r, at_y(DY[j]))
 
     def do_gz():
-        for j in range(3):
-            got(ary.at[j], gy_r.at[j])
+        got(ary.at[0:3], gy_r)
         ary[3] = msg[...] + ary[0] + ary[1] + ary[2]
         for d in range(1, 8):
-            send(ary.at[3], arz.at[d - 1], gz_s.at[d - 1], gz_r.at[d - 1], at_z(d))
-
-    def do_gx():
-        g = ary[3]
-        for d in range(7):
-            got(arz.at[d], gz_r.at[d])
-            g = g + arz[d]
-        gxs[...] = g
-        for i, dx in enumerate((1, 3, 2)):
-            b = ((x + dx) % 4) // 2
-            send(gxs.at[b], gxr.at[i], gx_s.at[i], gx_r.at[i], at_x(dx))
+            send(ary.at[3], arz.at[d - 1], SEND_S, gz_r, at_z(d))
 
     def total_inverse():
         tot = tsum2[...]
@@ -531,16 +520,17 @@
         return 1.0 / jnp.sum(jnp.sum(tot, axis=1, keepdims=True), axis=0, keepdims=True)
 
     def do_gf():
-        for i in range(3):
-            got(gxr.at[i], gx_r.at[i])
-        o_gg[...] = (gxs[xh] + gxr[0] + gxr[1] + gxr[2]) * inv_total
-        o_loss[...] = jnp.sum(gxs[2], axis=1, keepdims=True) * inv_total
+        got(arz, gz_r)
+        g = ary[3]
+        for d in range(7):
+            g = g + arz[d]
+        o_gg[...] = g[:, 0:1024] * inv_total
+        o_loss[...] = jnp.sum(g[:, 1024:1152], axis=1, keepdims=True) * inv_total
         result(o_loss, r_loss, 0)
         result(o_gg, r_gg, 1)
 
     def do_qt():
-        for i in range(7):
-            got(qt.at[peer_was(i)], qt_r.at[i])
+        got(qt.at[0:7], qt_r)
         qsum = qt[0]
         for i in range(1, 8):
             qsum = qsum + qt[i]
@@ -553,7 +543,7 @@
         ft = jnp.transpose(v)
         for a in range(2):
             ghs[a, :, PARTS[i]] = ft[a * 64:(a + 1) * 64]
-        send(ghs.at[1 - xl, :, PARTS[i]], ghr.at[:, PARTS[i]], fx_s.at[i], fx_r.at[i], mate)
+        send(ghs.at[1 - xl, :, PARTS[i]], ghr.at[:, PARTS[i]], SEND_S, fx_r.at[i], mate)
 
     def do_af():
         va = a_sum(0)
@@ -564,21 +554,22 @@
         turn(0, fa[...])
 
     def do_bf(q):
-        v = ght[0, :, qrows(q), :]
+        v = b_rows(0, q)
         for s in range(2):
             got(rbb.at[s, q, 0], rb_r.at[s, q, 0])
-            v = v + rbb[s, q, 0].astype(F32)
-        syb[q] = v
+            v = [v[b] + rbb[s, q, 0, b].astype(F32) for b in range(4)]
+        for b in range(4):
+            syb[q, b] = v[b]
         for j in range(3):
             src = syb.at[q, yy(DY[j])]
-            send(src, ryb.at[q, j], ry_s.at[q, j], ry_r.at[q, j], at_y(DY[j]))
+            send(src, ryb.at[q, j], SEND_S, ry_r.at[q], at_y(DY[j]))
 
     def do_bg(p):
         for h in range(2):
             q = 2 * p + h
             v = syb[q, y]
+            got(ryb.at[q], ry_r.at[q])
             for j in range(3):
-                got(ryb.at[q, j], ry_r.at[q, j])
                 v = v + ryb[q, j]
             fb[p, h * 64:(h + 1) * 64, :] = v
         turn(1 + p, fb[p])
@@ -620,22 +611,18 @@
         steps[name](*arg)
         if name == "tz" and arg[0] == 4:
             inv_total = total_inverse()
-    for cp in sent:
-        cp.wait_send()
+    for group, size in enumerate(sent):
+        whole = ght.at[pl.ds(0, size // 512)]
+        rc(whole, whole, send_s.at[group], send_s.at[group], at_y(1)).wait_send()
     for cp in results:
         cp.wait()
 
 
 def finish(*refs):
-    ins, outs, bufs, sem_in, sem_out = refs[0:4], refs[4:8], refs[8:12], refs[12], refs[13]
-    first = [pltpu.make_async_copy(ins[i], bufs[i], sem_in.at[i]) for i in range(4)]
-    second = [pltpu.make_async_copy(bufs[i], outs[i], sem_out.at[i]) for i in range(4)]
-    for cp in first:
+    copies = [pltpu.make_async_copy(refs[i], refs[4 + i], refs[8].at[i]) for i in range(4)]
+    for cp in copies:
         cp.start()
-    for one, two in zip(first, second):
-        one.wait()
-        two.start()
-    for cp in second:
+    for cp in copies:
         cp.wait()
 
 
@@ -668,7 +655,7 @@
         V((8, 4, 8, 128), F32),
         V((512, 128), F32),
         V((512, 128), F32),
-        V((8, 4, 512, 128), F32),
+        V((16384, 128), F32),
         V((8, 3, 256, 128), BF16),
         V((8, 3, 256, 128), BF16),
         V((2, 128, 128), BF16),
@@ -694,27 +681,25 @@
         V((2, 128, 1024), BF16),
         V((2, 128, 1024), F32),
         V((4, 1, 1024), F32),
+        V((2, 1, 1024), F32),
         V((3, 1, 1024), F32),
-        V((3, 1, 1024), F32),
-        V((3, 1, 1024), F32),
-        V((4, 3, 1, 1024), F32),
-        V((7, 3, 1, 1024), F32),
+        V((1, 1152), F32),
+        V((4, 1, 1152), F32),
+        V((7, 1, 1152), F32),
         V((8, 128), F32),
         V((8, 128), F32),
         V((3, 8, 128), F32),
         V((2, 4, 8, 128), F32),
         S((5,)),
         S((4,)),
+        S((3,)),
     ]
     shapes = [
-        (), (), (3,), (4,), (2,), (3,),
-        (2, 4), (8, 3), (3,), (2, 4, 4),
-        (7,), (7,), (3,), (2, 4),
-        (8, 3), (2, 4), (2, 4, 4), (4, 3), (3,),
-        (4,), (2,), (2,), (2,), (3,), (3,), (7,),
+        (), (), (), (4,), (2,), (3,), (2, 4), (8,), (3,), (2, 4, 4),
+        (), (), (), (2, 4), (8,), (2, 4), (2, 4, 4), (4,), (3,),
+        (4,), (2,), (2,), (2,), (), (), (),
     ]
-    for sh in shapes:
-        scratch += [S(sh), S(sh)] if sh else [S, S]
+    scratch += [S(sh) if sh else S for sh in shapes]
     loss, gh, gg, gx = pl.pallas_call(
         kernel,
         out_shape=(
@@ -723,20 +708,23 @@
             jax.ShapeDtypeStruct((1, 1024), F32),
             jax.ShapeDtypeStruct((256, 1024), BF16),
         ),
-        in_specs=[hbm] * 5,
+        in_specs=[pl.BlockSpec(memory_space=pltpu.HBM)] * 5,
         out_specs=(hbm,) * 4,
         scratch_shapes=scratch,
         compiler_params=pltpu.CompilerParams(
-            collective_id=0, has_side_effects=True, vmem_limit_bytes=62 << 20
+            collective_id=0, has_side_effects=True, vmem_limit_bytes=53 << 20
         ),
-    )(hidden, gain.reshape(1, 1024), head, targets.reshape(2, 128), row_weight.reshape(2, 128))
+    )(*[
+        pltpu.with_memory_space_constraint(a, pltpu.HBM)
+        for a in (hidden, gain.reshape(1, 1024), head, targets.reshape(2, 128), row_weight.reshape(2, 128))
+    ])
     loss, gh, gg, gx = pl.pallas_call(
         finish,
         out_shape=tuple(jax.ShapeDtypeStruct(a.shape, a.dtype) for a in (loss, gh, gg, gx)),
         in_specs=[hbm] * 4,
         out_specs=(hbm,) * 4,
-        scratch_shapes=[V(a.shape, a.dtype) for a in (loss, gh, gg, gx)] + [S((4,)), S((4,))],
-        compiler_params=pltpu.CompilerParams(vmem_limit_bytes=62 << 20),
+        scratch_shapes=[S((4,))],
+        compiler_params=pltpu.CompilerParams(vmem_limit_bytes=2 << 20),
     )(loss, gh, gg, gx)
     return (loss.reshape(()), gh, gg.reshape(1024), gx)
 

time: 94.5 us -> 88 us (0.931)
  Pallas kernels: 93.7 us -> 86.9 us
    pallas_call x1, Pallas kernels: 91.1 us -> 85.3 us  [body(): pl.pallas_call(kernel, out_shape=(jax.ShapeDtypeStruct((1, 1), F32), jax....]
    pallas_call x1, Pallas kernels: 2.62 us -> 1.56 us  [body(): pl.pallas_call(finish, out_shape=tuple((jax.ShapeDtypeStruct(a.shape, a.d...]
where the time goes in v3:
time: 88 us; the launch traced here: 87.5 us
  Pallas kernels  86.9 us (99%)
    pallas_call x1, Pallas kernels, body(): pl.pallas_call(kernel, out_shape=(jax.ShapeDtypeStruct((1, 1), F32), jax....  85.3 us

profile of v3, /device:TPU:2, one launch (start us, length us, event | category | flops | bytes accessed | tf_op | source)
XLA Modules:
  0.0 87.5 jit_solution(18351345984842003237)
XLA Ops:
  0.6 85.3 %shard_map.84 = (f32[1,1]{1,0:T(1,128)}, f32[64,1024]{1,0:T(8,128)S(1)}, f32[1,1024]{1,0:T(1,128)S(1)}, bf16[256,1024]{1,0:T(8,128)(2,1)S(1)}) custom-call(bf16[256,1024]{1,0:T(8,128)(2,1)} %hid.1, f32[1,1024]{1,0:T(1,128)} %bitcast.5, bf16[64,1024]{1,0:T(8,128)(2,1)} %hin_hbm.1, s32[2,128]{1,0:T(2,128)} %bitcast.6, s32[2,128]{1,0:T(2,128)} %bitcast.7), custom_call_target="tpu_custom_call" | custom-call | tf_op jit(solution)/shard_map/pallas_call | solution.py:703
  86.0 1.6 %shard_map.85 = (f32[1,1]{1,0:T(1,128)}, f32[64,1024]{1,0:T(8,128)}, f32[1,1024]{1,0:T(1,128)}, bf16[256,1024]{1,0:T(8,128)(2,1)}) custom-call(f32[1,1]{1,0:T(1,128)} %get-tuple-element.12.refs_0_, f32[64,1024]{1,0:T(8,128)S(1)} %get-tuple-element.13.refs_1_, f32[1,1024]{1,0:T(1,128)S(1)} %get-tuple-element.14.refs_2_, ...), custom_call_target="tpu_custom_call" | custom-call | tf_op jit(solution)/shard_map/pallas_call | solution.py:721

commit v4 on v3

--- a/solution.py
+++ b/solution.py
@@ -17,9 +17,9 @@
 SZ = (1, 7)
 PEERS = ((1, 0), (3, 0), (2, 0), (0, 1), (1, 1), (3, 1), (2, 1))
 GATHER = (
-    ("xe",), ("by", 1), ("bz", 0, 1, 0), ("bz", 1, 1, 0), ("by", 2), ("az", 0, 1), ("az", 1, 1), ("xo",),
-    ("bz", 0, 1, 1), ("bz", 1, 1, 1), ("bz", 0, 2, 0), ("bz", 1, 2, 0), ("xf", 1), ("xf", 0), ("by", 3),
-    ("az", 0, 2), ("az", 1, 2), ("xs", 1), ("xs", 0), ("ty",), ("bz", 0, 1, 2), ("bz", 1, 1, 2), ("iv", 1),
+    ("xe",), ("by", 1), ("bz", 0, 1, 0), ("bz", 1, 1, 0), ("az", 0, 1), ("az", 1, 1), ("by", 2), ("xo",),
+    ("bz", 0, 1, 1), ("bz", 1, 1, 1), ("bz", 0, 2, 0), ("bz", 1, 2, 0), ("xf", 1), ("xf", 0),
+    ("az", 0, 2), ("az", 1, 2), ("by", 3), ("xs", 1), ("xs", 0), ("ty",), ("bz", 0, 1, 2), ("bz", 1, 1, 2), ("iv", 1),
     ("nm", 1, 0), ("nm", 1, 1), ("nm", 1, 2), ("nm", 1, 3), ("bz", 0, 2, 1), ("bz", 1, 2, 1), ("nm", 1, 4),
     ("nm", 1, 5), ("nm", 1, 6), ("nm", 1, 7), ("bz", 0, 3, 0), ("bz", 1, 3, 0), ("az", 0, 3), ("az", 1, 3),
     ("bz", 0, 1, 3), ("bz", 1, 1, 3), ("bz", 0, 2, 2), ("bz", 1, 2, 2), ("xf", 2), ("bz", 0, 3, 1), ("bz", 1, 3, 1),
@@ -29,15 +29,16 @@
     ("lg", 2), ("bz", 0, 4, 1), ("lg", 3), ("bz", 0, 3, 3), ("bz", 1, 4, 3), ("lg", 5), ("lg", 4),
 )
 SCATTER = (
-    ("hg", 4), ("bc", 0, 4, 0), ("bc", 1, 4, 1), ("bc", 0, 4, 2), ("bc", 1, 4, 3), ("hg", 3), ("bc", 0, 3, 1),
-    ("bc", 0, 3, 3), ("hg", 5), ("bc", 1, 3, 0), ("bc", 1, 3, 2), ("ds", 0), ("hg", 2), ("ds", 1), ("du", 0),
-    ("bc", 0, 3, 0), ("bc", 1, 3, 1), ("ds", 2), ("bc", 0, 3, 2), ("bc", 1, 3, 3), ("hg", 6), ("a4",), ("du", 1),
-    ("bc", 0, 2, 1), ("bc", 1, 2, 0), ("ds", 3), ("du", 2), ("bc", 0, 2, 3), ("bc", 1, 2, 2), ("du", 3), ("gx",),
-    ("hg", 1), ("bc", 0, 2, 0), ("bc", 1, 2, 1), ("hg", 7), ("hg", 0), ("xr", 1), ("xr", 2), ("ac", 0, 3),
-    ("ac", 1, 3), ("bc", 0, 2, 2), ("bc", 1, 2, 3), ("bc", 0, 1, 1), ("bc", 1, 1, 0), ("tz", 3), ("bc", 0, 1, 3),
-    ("bc", 1, 1, 2), ("bc", 0, 1, 0), ("bc", 1, 1, 1), ("bc", 0, 1, 2), ("bc", 1, 1, 3), ("ac", 0, 2),
-    ("ac", 1, 2), ("gy",), ("tz", 4), ("qt",), ("bf", 0), ("bf", 1), ("ac", 0, 1), ("ac", 1, 1), ("gz",), ("bf", 2),
-    ("bf", 3), ("bg", 0), ("bg", 1), ("af",), ("fi",), ("gf",), ("gh",),
+    ("hg", 4), ("ai", 4), ("bc", 0, 4, 0), ("bc", 1, 4, 1), ("hg", 3), ("ai", 3), ("bc", 0, 3, 1), ("ds", 0),
+    ("hg", 5), ("ai", 5), ("bc", 1, 3, 0), ("bc", 0, 4, 2), ("bc", 1, 4, 2), ("ds", 1), ("du", 0), ("ds", 2),
+    ("yr", 4), ("bc", 0, 3, 0), ("bc", 1, 3, 1), ("hg", 2), ("ai", 2), ("yr", 3), ("du", 1), ("bc", 0, 2, 1),
+    ("hg", 6), ("ai", 6), ("yr", 5), ("bc", 1, 2, 0), ("bc", 0, 3, 2), ("bc", 1, 3, 2), ("ds", 3), ("du", 2),
+    ("hg", 1), ("ai", 1), ("a4",), ("bc", 0, 2, 0), ("bc", 1, 2, 1), ("hg", 0), ("ai", 0), ("hg", 7), ("ai", 7),
+    ("du", 3), ("yr", 2), ("gx",), ("qs",), ("bc", 0, 1, 1), ("bc", 1, 1, 0), ("bc", 0, 2, 2), ("bc", 1, 2, 2),
+    ("xr", 1), ("xr", 2), ("yr", 6), ("ac", 0, 3), ("ac", 1, 3), ("bc", 0, 1, 0), ("bc", 1, 1, 1), ("yr", 1),
+    ("yr", 7), ("yr", 0), ("tz", 3), ("ac", 0, 2), ("bc", 0, 1, 2), ("bc", 1, 1, 2), ("ac", 1, 2), ("qt",), ("gy",),
+    ("bf", 0), ("bf", 1), ("tz", 4), ("bf", 2), ("al",), ("gz",), ("bg",), ("fi",), ("af", 0), ("af", 1), ("bm",),
+    ("gf",), ("gh",),
 )
 
 
@@ -45,12 +46,12 @@
     hid, gain, hin_hbm, tgt_hbm, wgt_hbm,
     r_loss, r_gh, r_gg, r_hid,
     tgt, wgt, o_loss, o_gh, o_gg, o_hid, hin, hb, xg, nm, gg4, tw, ssq, invb, tgtb, wb, lg, ex, dl, dlt,
-    st, qt, lseb, stat,
-    ght, sba, rba, sa4, ra4, sa3, ra3, sa2, ra2, sbb, rbb, syb, ryb, fa, fb, ghs, ghr,
+    st, qt, lseb, stat, pick, lser,
+    ght, sbf, rbf, sba, rba, sa4, ra4, sa3, ra3, sa2, ra2, sb4, rb4, sbb, rbb, syb, ryb, fa, fb, ghs, ghr,
     dno, dns, dnr, dxs, dxr, dos, dor, rbx, gps, gxs, gxr, msg, ary, arz, tsum, tsum2, tot_y, tot_z,
     in_s, out_s, send_s,
     xh_r, tw_r, gn_r, hx_r, hh_r, hf_r, az_r, ay_r, by_r, bz_r, st_r, qt_r, ty_r, tz_r,
-    ra_r, rz_r, rb_r, ry_r, fx_r, dc_r, d2_r, dx_r, do_r, gx_r, gy_r, gz_r,
+    rf_r, ra_r, rz_r, rl_r, rb_r, ry_r, fx_r, dc_r, d2_r, dx_r, do_r, gx_r, gy_r, gz_r,
 ):
     f = lax.axis_index("fsdp")
     t = lax.axis_index("tp")
@@ -324,12 +325,8 @@
         ev = jnp.exp(l - m)
         ex[rows, :] = ev
         e = jnp.sum(ev, axis=1, keepdims=True)
-        a = i // 8
-        tb = tgtb[a, pl.ds(pl.multiple_of((i % 8) * 32, 32), 32), :][:, 0:1] - col0
-        cols = lax.broadcasted_iota(jnp.int32, (32, 512), 1).astype(F32)
-        pk = jnp.sum(jnp.where(cols == tb, l, 0.0), axis=1, keepdims=True)
         lane = lax.broadcasted_iota(jnp.int32, (32, 128), 1)
-        stat[rows, :] = jnp.where(lane == 0, m, jnp.where(lane == 1, e, jnp.where(lane == 2, pk, 0.0)))
+        stat[rows, :] = jnp.where(lane == 0, m, jnp.where(lane == 1, e, 0.0))
         return carry
 
     lax.fori_loop(0, 16, stat_step, 0, unroll=4)
@@ -338,94 +335,140 @@
     for i, (dx, dc) in enumerate(PEERS):
         send(st.at[me], st.at[me], SEND_S, st_r, at_x(dx, dc))
 
+    def pick_step(i, carry):
+        rows = pl.ds(pl.multiple_of(i * 32, 32), 32)
+        a = i // 8
+        tb = tgtb[a, pl.ds(pl.multiple_of((i % 8) * 32, 32), 32), :][:, 0:1] - col0
+        cols = lax.broadcasted_iota(jnp.int32, (32, 512), 1).astype(F32)
+        pk = jnp.sum(jnp.where(cols == tb, lg[rows, :], 0.0), axis=1, keepdims=True)
+        pick[rows, :] = jnp.broadcast_to(pk, (32, 128))
+        return carry
+
+    lax.fori_loop(0, 16, pick_step, 0, unroll=4)
     got(st.at[0:7], st_r)
     allst = st[...]
     mx = jnp.max(allst[:, :, 0:1, :], axis=0)
     es = jnp.sum(allst[:, :, 1:2, :] * jnp.exp(allst[:, :, 0:1, :] - mx[None]), axis=0)
-    pk = jnp.sum(allst[:, :, 2:3, :], axis=0)
     lse = mx + jnp.log(es)
-    loss_row = jnp.zeros((1, 128), F32)
+    lser[...] = lse
     for k in range(4):
-        loss_row = loss_row + tw[k // 2, 2 + k % 2:3 + k % 2, :] * (lse[k] - pk[k])
         lseb[k * 128:(k + 1) * 128, :] = col(lse[k])
 
     def dl_step(i, carry):
         a = i // 8
         rows = pl.ds(pl.multiple_of((i % 8) * 32, 32), 32)
         g = pl.ds(pl.multiple_of(i * 32, 32), 32)
-        l = lg[g, :]
         tb = tgtb[a, rows, :][:, 0:1] - col0
         w = wb[a, rows, :][:, 0:1]
         cols = lax.broadcasted_iota(jnp.int32, (32, 512), 1).astype(F32)
         p = ex[g, :] * jnp.exp(stat[g, :][:, 0:1] - lseb[g, :][:, 0:1])
         d = (w * (p - jnp.where(cols == tb, 1.0, 0.0))).astype(BF16)
         dl[a, rows, :] = d
-        q = jnp.sum(d.astype(F32) * l, axis=1, keepdims=True)
-        stat[g, :] = jnp.broadcast_to(q, (32, 128))
         return carry
 
     lax.fori_loop(0, 16, dl_step, 0, unroll=4)
     for a in range(2):
         dlt[:, a * 256:(a + 1) * 256] = jnp.transpose(dl[a])
 
-    for k in range(4):
-        qt[me, k] = jnp.transpose(stat[k * 128:(k + 1) * 128, :])[0:8, :]
-    for i, (dx, dc) in enumerate(PEERS):
-        send(qt.at[me], qt.at[me], SEND_S, qt_r, at_x(dx, dc))
-
-    def a_rows(k, b):
-        return pl.ds(pl.multiple_of((k * 4 + b) * 512, 512), 256)
+    def do_qs():
+        def step(i, carry):
+            a = i // 8
+            g = pl.ds(pl.multiple_of(i * 32, 32), 32)
+            d = dl[a, pl.ds(pl.multiple_of((i % 8) * 32, 32), 32), :]
+            q = jnp.sum(d.astype(F32) * lg[g, :], axis=1, keepdims=True)
+            lane = lax.broadcasted_iota(jnp.int32, (32, 128), 1)
+            stat[g, :] = jnp.where(lane == 0, q, pick[g, :])
+            return carry
+        lax.fori_loop(0, 16, step, 0, unroll=4)
+        for k in range(4):
+            qt[me, k] = jnp.transpose(stat[k * 128:(k + 1) * 128, :])[0:8, :]
+        for i, (dx, dc) in enumerate(PEERS):
+            send(qt.at[me], qt.at[me], SEND_S, qt_r, at_x(dx, dc))
+
+    def a_rows(k, b, h):
+        return pl.ds(pl.multiple_of((k * 4 + b) * 512 + h * 160, 32), 160)
+
+    Q_AT = (384, 448, 320)
 
     def b_rows(k, q):
-        return [ght[(k * 4 + b) * 512 + 256 + q * 64:(k * 4 + b) * 512 + 320 + q * 64, :] for b in range(4)]
+        first = Q_AT[q]
+        return [ght[(k * 4 + b) * 512 + first:(k * 4 + b) * 512 + first + 64, :] for b in range(4)]
 
     def do_hg(k):
         g = jnp.dot(dlt[...], nm[zz(k)], preferred_element_type=F32)
         for b in range(4):
             ght[(k * 4 + b) * 512:(k * 4 + b + 1) * 512, :] = g[:, b * 128:(b + 1) * 128]
-        for j in range(3):
-            sba[k, j] = ght[a_rows(k, yy(DY[j])), :].astype(BF16)
-            send(sba.at[k, j], rba.at[k, j], SEND_S, ra_r.at[k], at_y(DY[j]))
+        for i in range(2):
+            sbf[k, i] = ght[a_rows(k, yy(2), i), :].astype(BF16)
+            send(sbf.at[k, i], rbf.at[k, i], SEND_S, rf_r.at[k], at_y(DY[i]))
+
+    def do_ai(k):
+        for i in range(2):
+            sba[k, i, 1 - i] = ght[a_rows(k, yy(DY[i]), 1 - i), :].astype(BF16)
+            send(sba.at[k, i, 1 - i], rba.at[k, i, 1 - i], SEND_S, ra_r.at[k, 0], at_y(DY[i]))
+
+    def do_yr(k):
+        got(rbf.at[k], rf_r.at[k])
+        for i in range(2):
+            sba[k, i, i] = (ght[a_rows(k, yy(DY[i]), i), :] + rbf[k, i].astype(F32)).astype(BF16)
+            send(sba.at[k, i, i], rba.at[k, i, i], SEND_S, ra_r.at[k, 1], at_y(DY[i]))
 
     def do_bc(s, d, q):
         v = b_rows((SZ[s] * d) % 8, q)
-        if d < (4 if q % 2 == s else 3):
-            got(rbb.at[s, q, d], rb_r.at[s, q, d])
-            v = [v[b] + rbb[s, q, d, b].astype(F32) for b in range(4)]
-        for b in range(4):
-            sbb[s, q, d - 1, b] = v[b].astype(BF16)
+        h = slice(s * 32, (s + 1) * 32)
+        if q == 2 and d == 4:
+            for b in range(4):
+                sb4[s, b] = v[b][h].astype(BF16)
+            send(sb4.at[s], rb4.at[s], SEND_S, rb_r.at[s, q, 3], at_z(SZ[s]))
+            return
+        if q == 2 and d == 3:
+            got(rb4.at[s], rb_r.at[s, q, 3])
+            for b in range(4):
+                sbb[s, q, 2, b] = v[b].astype(BF16)
+                sbb[s, q, 2, b, h] = (v[b][h] + rb4[s, b].astype(F32)).astype(BF16)
+        else:
+            if d < (4 if q == s else 3):
+                got(rbb.at[s, q, d], rb_r.at[s, q, d])
+                v = [v[b] + rbb[s, q, d, b].astype(F32) for b in range(4)]
+            for b in range(4):
+                sbb[s, q, d - 1, b] = v[b].astype(BF16)
         send(sbb.at[s, q, d - 1], rbb.at[s, q, d - 1], SEND_S, rb_r.at[s, q, d - 1], at_z(SZ[s]))
 
     def a_sum(k):
-        v = ght[a_rows(k, y), :]
-        got(rba.at[k], ra_r.at[k])
-        for j in range(3):
-            v = v + rba[k, j].astype(F32)
-        return v
+        for i in range(2):
+            got(rba.at[k, 0], ra_r.at[k, i])
+        return [
+            ght[a_rows(k, y, h), :] + rba[k, 0, h].astype(F32) + rba[k, 1, h].astype(F32) for h in range(2)
+        ]
 
     def do_a4():
-        fa[...] = a_sum(4)
+        v = a_sum(4)
         for s in range(2):
-            h = slice(s * 128, (s + 1) * 128)
-            sa4[s] = fa[h, :].astype(BF16)
+            sa4[s] = v[s].astype(BF16)
             send(sa4.at[s], ra4.at[s], SEND_S, rz_r.at[s, 3], at_z(SZ[s]))
 
     def do_ac(s, d):
         v = a_sum((SZ[s] * d) % 8)
         if d == 3:
-            h = slice(s * 128, (s + 1) * 128)
-            sa3[s] = v.astype(BF16)
             got(ra4.at[s], rz_r.at[s, 3])
-            sa3[s, h] = (v[h] + ra4[s].astype(F32)).astype(BF16)
+            v[s] = v[s] + ra4[s].astype(F32)
+            for h in range(2):
+                sa3[s, h] = v[h].astype(BF16)
             send(sa3.at[s], ra3.at[s], SEND_S, rz_r.at[s, 2], at_z(SZ[s]))
             return
-        if d == 2:
-            got(ra3.at[s], rz_r.at[s, 2])
-            sa2[s, 1] = v + ra3[s].astype(F32)
-        else:
+        got(ra3.at[s], rz_r.at[s, 2])
+        for h in range(2):
+            sa2[s, 1, h] = v[h] + ra3[s, h].astype(F32)
+        send(sa2.at[s, 1], ra2.at[s, 1], SEND_S, rz_r.at[s, 1], at_z(SZ[s]))
+
+    def do_al():
+        for s in range(2):
             got(ra2.at[s, 1], rz_r.at[s, 1])
-            sa2[s, 0] = v + ra2[s, 1]
-        send(sa2.at[s, d - 1], ra2.at[s, d - 1], SEND_S, rz_r.at[s, d - 1], at_z(SZ[s]))
+        v = [a_sum(SZ[s]) for s in range(2)]
+        for h in range(2):
+            for s in range(2):
+                sa2[s, 0, h] = v[s][h] + ra2[s, 1, h]
+                send(sa2.at[s, 0, h], ra2.at[s, 0, h], SEND_S, rl_r.at[s, h], at_z(SZ[s]))
 
     XO = (2, 1, 3, 0)
 
@@ -502,7 +545,6 @@
     def do_gy():
         got(gxr, gx_r)
         msg[:, 0:1024] = gxs[xh] + gxr[0] + gxr[1] + gxr[2]
-        msg[:, 1024:1152] = loss_row
         for j in range(3):
             send(msg, ary.at[j], SEND_S, gy_r, at_y(DY[j]))
 
@@ -534,10 +576,13 @@
         qsum = qt[0]
         for i in range(1, 8):
             qsum = qsum + qt[i]
+        loss_row = jnp.zeros((1, 128), F32)
         for k in range(4):
+            loss_row = loss_row + tw[k // 2, 2 + k % 2:3 + k % 2, :] * (lser[k] - qsum[k, 1:2, :])
             lseb[k * 128:(k + 1) * 128, :] = col(qsum[k, 0:1, :])
-
-    PARTS = (slice(0, 256), slice(256, 384), slice(384, 512))
+        msg[:, 1024:1152] = loss_row
+
+    PARTS = tuple(slice(i * 128, (i + 1) * 128) for i in range(4))
 
     def turn(i, v):
         ft = jnp.transpose(v)
@@ -545,13 +590,16 @@
             ghs[a, :, PARTS[i]] = ft[a * 64:(a + 1) * 64]
         send(ghs.at[1 - xl, :, PARTS[i]], ghr.at[:, PARTS[i]], SEND_S, fx_r.at[i], mate)
 
-    def do_af():
-        va = a_sum(0)
+    def do_af(h):
+        if h == 0:
+            for i in range(2):
+                got(rba.at[0, 0], ra_r.at[0, i])
+        v = ght[a_rows(0, y, h), :] + rba[0, 0, h].astype(F32) + rba[0, 1, h].astype(F32)
         for s in range(2):
-            got(ra2.at[s, 0], rz_r.at[s, 0])
-            va = va + ra2[s, 0]
-        fa[...] = va
-        turn(0, fa[...])
+            got(ra2.at[s, 0, h], rl_r.at[s, h])
+            v = v + ra2[s, 0, h]
+        fa[h * 160:(h + 1) * 160, :] = v
+        turn(h, fa[h * 128:(h + 1) * 128, :])
 
     def do_bf(q):
         v = b_rows(0, q)
@@ -564,19 +612,25 @@
             src = syb.at[q, yy(DY[j])]
             send(src, ryb.at[q, j], SEND_S, ry_r.at[q], at_y(DY[j]))
 
-    def do_bg(p):
-        for h in range(2):
-            q = 2 * p + h
-            v = syb[q, y]
-            got(ryb.at[q], ry_r.at[q])
-            for j in range(3):
-                v = v + ryb[q, j]
-            fb[p, h * 64:(h + 1) * 64, :] = v
-        turn(1 + p, fb[p])
+    def b_sum(q):
+        v = syb[q, y]
+        got(ryb.at[q], ry_r.at[q])
+        for j in range(3):
+            v = v + ryb[q, j]
+        return v
+
+    def do_bg():
+        for q in range(2):
+            fb[q * 64:(q + 1) * 64, :] = b_sum(q)
+        turn(3, fb[...])
+
+    def do_bm():
+        fa[320:384, :] = b_sum(2)
+        turn(2, fa[256:384, :])
 
     def do_gh():
         o_gh[:, pl.ds(own, 512)] = ghs[xl] * inv_total
-        for i in range(3):
+        for i in range(4):
             got(ghr.at[:, PARTS[i]], fx_r.at[i])
         o_gh[:, pl.ds(oth, 512)] = ghr[...] * inv_total
         result(o_gh, r_gh, 2)
@@ -605,7 +659,7 @@
 
     steps = dict(
         ds=do_ds, hg=do_hg, bc=do_bc, du=do_du, a4=do_a4, ac=do_ac, xr=do_xr, gy=do_gy, gz=do_gz,
-        gx=do_gx, gf=do_gf, qt=do_qt, tz=do_tz, af=do_af, bf=do_bf, bg=do_bg, gh=do_gh, fi=do_fi,
+        gx=do_gx, gf=do_gf, qs=do_qs, qt=do_qt, tz=do_tz, yr=do_yr, ai=do_ai, al=do_al, af=do_af, bf=do_bf, bg=do_bg, bm=do_bm, gh=do_gh, fi=do_fi,
     )
     for name, *arg in SCATTER:
         steps[name](*arg)
@@ -655,21 +709,27 @@
         V((8, 4, 8, 128), F32),
         V((512, 128), F32),
         V((512, 128), F32),
+        V((512, 128), F32),
+        V((4, 1, 128), F32),
         V((16384, 128), F32),
-        V((8, 3, 256, 128), BF16),
-        V((8, 3, 256, 128), BF16),
-        V((2, 128, 128), BF16),
-        V((2, 128, 128), BF16),
-        V((2, 256, 128), BF16),
-        V((2, 256, 128), BF16),
-        V((2, 2, 256, 128), F32),
-        V((2, 2, 256, 128), F32),
-        V((2, 4, 4, 4, 64, 128), BF16),
-        V((2, 4, 4, 4, 64, 128), BF16),
-        V((4, 4, 64, 128), F32),
-        V((4, 3, 64, 128), F32),
-        V((256, 128), F32),
-        V((2, 128, 128), F32),
+        V((8, 2, 160, 128), BF16),
+        V((8, 2, 160, 128), BF16),
+        V((8, 2, 2, 160, 128), BF16),
+        V((8, 2, 2, 160, 128), BF16),
+        V((2, 160, 128), BF16),
+        V((2, 160, 128), BF16),
+        V((2, 2, 160, 128), BF16),
+        V((2, 2, 160, 128), BF16),
+        V((2, 2, 2, 160, 128), F32),
+        V((2, 2, 2, 160, 128), F32),
+        V((2, 4, 32, 128), BF16),
+        V((2, 4, 32, 128), BF16),
+        V((2, 3, 4, 4, 64, 128), BF16),
+        V((2, 3, 4, 4, 64, 128), BF16),
+        V((3, 4, 64, 128), F32),
+        V((3, 3, 64, 128), F32),
+        V((384, 128), F32),
+        V((128, 128), F32),
         V((2, 64, 512), F32),
         V((64, 512), F32),
         V((4, 256, 1024), F32),
@@ -696,7 +756,7 @@
     ]
     shapes = [
         (), (), (), (4,), (2,), (3,), (2, 4), (8,), (3,), (2, 4, 4),
-        (), (), (), (2, 4), (8,), (2, 4), (2, 4, 4), (4,), (3,),
+        (), (), (), (2, 4), (8,), (8, 2), (2, 4), (2, 2), (2, 3, 4), (3,), (4,),
         (4,), (2,), (2,), (2,), (), (), (),
     ]
     scratch += [S(sh) if sh else S for sh in shapes]

time: 88 us -> 87.1 us (0.990)
  no operation moved by 1% of the time
where the time goes in v4:
time: 87.1 us; the launch traced here: 86.8 us
  Pallas kernels  86.2 us (99%)
    pallas_call x1, Pallas kernels, body(): pl.pallas_call(kernel, out_shape=(jax.ShapeDtypeStruct((1, 1), F32), jax....  84.6 us

profile of v4, /device:TPU:2, one launch (start us, length us, event | category | flops | bytes accessed | tf_op | source)
XLA Modules:
  0.0 86.8 jit_solution(11904809841841975438)
XLA Ops:
  0.6 84.6 %shard_map.84 = (f32[1,1]{1,0:T(1,128)}, f32[64,1024]{1,0:T(8,128)S(1)}, f32[1,1024]{1,0:T(1,128)S(1)}, bf16[256,1024]{1,0:T(8,128)(2,1)S(1)}) custom-call(bf16[256,1024]{1,0:T(8,128)(2,1)} %hid.1, f32[1,1024]{1,0:T(1,128)} %bitcast.5, bf16[64,1024]{1,0:T(8,128)(2,1)} %hin_hbm.1, s32[2,128]{1,0:T(2,128)} %bitcast.6, s32[2,128]{1,0:T(2,128)} %bitcast.7), custom_call_target="tpu_custom_call" | custom-call | tf_op jit(solution)/shard_map/pallas_call | solution.py:763
  85.3 1.6 %shard_map.85 = (f32[1,1]{1,0:T(1,128)}, f32[64,1024]{1,0:T(8,128)}, f32[1,1024]{1,0:T(1,128)}, bf16[256,1024]{1,0:T(8,128)(2,1)}) custom-call(f32[1,1]{1,0:T(1,128)} %get-tuple-element.12.refs_0_, f32[64,1024]{1,0:T(8,128)S(1)} %get-tuple-element.13.refs_1_, f32[1,1024]{1,0:T(1,128)S(1)} %get-tuple-element.14.refs_2_, ...), custom_call_target="tpu_custom_call" | custom-call | tf_op jit(solution)/shard_map/pallas_call | solution.py:781

commit v5 on v4

--- a/solution.py
+++ b/solution.py
@@ -30,15 +30,15 @@
 )
 SCATTER = (
     ("hg", 4), ("ai", 4), ("bc", 0, 4, 0), ("bc", 1, 4, 1), ("hg", 3), ("ai", 3), ("bc", 0, 3, 1), ("ds", 0),
-    ("hg", 5), ("ai", 5), ("bc", 1, 3, 0), ("bc", 0, 4, 2), ("bc", 1, 4, 2), ("ds", 1), ("du", 0), ("ds", 2),
-    ("yr", 4), ("bc", 0, 3, 0), ("bc", 1, 3, 1), ("hg", 2), ("ai", 2), ("yr", 3), ("du", 1), ("bc", 0, 2, 1),
-    ("hg", 6), ("ai", 6), ("yr", 5), ("bc", 1, 2, 0), ("bc", 0, 3, 2), ("bc", 1, 3, 2), ("ds", 3), ("du", 2),
-    ("hg", 1), ("ai", 1), ("a4",), ("bc", 0, 2, 0), ("bc", 1, 2, 1), ("hg", 0), ("ai", 0), ("hg", 7), ("ai", 7),
+    ("tz", 3), ("hg", 5), ("ai", 5), ("bc", 1, 3, 0), ("bc", 0, 4, 2), ("bc", 1, 4, 2), ("ds", 1), ("du", 0),
+    ("ds", 2), ("yr", 4), ("bc", 0, 3, 0), ("bc", 1, 3, 1), ("hg", 2), ("ai", 2), ("yr", 3), ("du", 1),
+    ("bc", 0, 2, 1), ("hg", 6), ("ai", 6), ("yr", 5), ("bc", 1, 2, 0), ("bc", 0, 3, 2), ("bc", 1, 3, 2), ("ds", 3),
+    ("tz", 4), ("a4",), ("du", 2), ("hg", 1), ("ai", 1), ("bc", 0, 2, 0), ("bc", 1, 2, 1), ("hg", 7), ("ai", 7),
     ("du", 3), ("yr", 2), ("gx",), ("qs",), ("bc", 0, 1, 1), ("bc", 1, 1, 0), ("bc", 0, 2, 2), ("bc", 1, 2, 2),
-    ("xr", 1), ("xr", 2), ("yr", 6), ("ac", 0, 3), ("ac", 1, 3), ("bc", 0, 1, 0), ("bc", 1, 1, 1), ("yr", 1),
-    ("yr", 7), ("yr", 0), ("tz", 3), ("ac", 0, 2), ("bc", 0, 1, 2), ("bc", 1, 1, 2), ("ac", 1, 2), ("qt",), ("gy",),
-    ("bf", 0), ("bf", 1), ("tz", 4), ("bf", 2), ("al",), ("gz",), ("bg",), ("fi",), ("af", 0), ("af", 1), ("bm",),
-    ("gf",), ("gh",),
+    ("xr", 1), ("xr", 2), ("yr", 6), ("ac", 0, 3), ("ac", 1, 3), ("hg", 0), ("ai", 0), ("bc", 0, 1, 0),
+    ("bc", 1, 1, 1), ("yr", 1), ("yr", 7), ("bc", 0, 1, 2), ("bc", 1, 1, 2), ("ac", 0, 2), ("ac", 1, 2), ("yr", 0),
+    ("qt",), ("gy",), ("bf", 0), ("bf", 1), ("al", 0), ("bf", 2), ("gz",), ("al", 1), ("bg",), ("af", 0), ("af", 1),
+    ("bm",), ("fi",), ("gf",), ("gh",),
 )
 
 
@@ -434,12 +434,16 @@
                 sbb[s, q, d - 1, b] = v[b].astype(BF16)
         send(sbb.at[s, q, d - 1], rbb.at[s, q, d - 1], SEND_S, rb_r.at[s, q, d - 1], at_z(SZ[s]))
 
-    def a_sum(k):
+    def a_wait(k):
         for i in range(2):
             got(rba.at[k, 0], ra_r.at[k, i])
-        return [
-            ght[a_rows(k, y, h), :] + rba[k, 0, h].astype(F32) + rba[k, 1, h].astype(F32) for h in range(2)
-        ]
+
+    def a_half(k, h):
+        return ght[a_rows(k, y, h), :] + rba[k, 0, h].astype(F32) + rba[k, 1, h].astype(F32)
+
+    def a_sum(k):
+        a_wait(k)
+        return [a_half(k, h) for h in range(2)]
 
     def do_a4():
         v = a_sum(4)
@@ -459,16 +463,15 @@
         got(ra3.at[s], rz_r.at[s, 2])
         for h in range(2):
             sa2[s, 1, h] = v[h] + ra3[s, h].astype(F32)
-        send(sa2.at[s, 1], ra2.at[s, 1], SEND_S, rz_r.at[s, 1], at_z(SZ[s]))
-
-    def do_al():
+            send(sa2.at[s, 1, h], ra2.at[s, 1, h], SEND_S, rl_r.at[s, 1, h], at_z(SZ[s]))
+
+    def do_al(h):
         for s in range(2):
-            got(ra2.at[s, 1], rz_r.at[s, 1])
-        v = [a_sum(SZ[s]) for s in range(2)]
-        for h in range(2):
-            for s in range(2):
-                sa2[s, 0, h] = v[s][h] + ra2[s, 1, h]
-                send(sa2.at[s, 0, h], ra2.at[s, 0, h], SEND_S, rl_r.at[s, h], at_z(SZ[s]))
+            if h == 0:
+                a_wait(SZ[s])
+            got(ra2.at[s, 1, h], rl_r.at[s, 1, h])
+            sa2[s, 0, h] = a_half(SZ[s], h) + ra2[s, 1, h]
+            send(sa2.at[s, 0, h], ra2.at[s, 0, h], SEND_S, rl_r.at[s, 0, h], at_z(SZ[s]))
 
     XO = (2, 1, 3, 0)
 
@@ -592,11 +595,10 @@
 
     def do_af(h):
         if h == 0:
-            for i in range(2):
-                got(rba.at[0, 0], ra_r.at[0, i])
-        v = ght[a_rows(0, y, h), :] + rba[0, 0, h].astype(F32) + rba[0, 1, h].astype(F32)
+            a_wait(0)
+        v = a_half(0, h)
         for s in range(2):
-            got(ra2.at[s, 0, h], rl_r.at[s, h])
+            got(ra2.at[s, 0, h], rl_r.at[s, 0, h])
             v = v + ra2[s, 0, h]
         fa[h * 160:(h + 1) * 160, :] = v
         turn(h, fa[h * 128:(h + 1) * 128, :])
@@ -756,7 +758,7 @@
     ]
     shapes = [
         (), (), (), (4,), (2,), (3,), (2, 4), (8,), (3,), (2, 4, 4),
-        (), (), (), (2, 4), (8,), (8, 2), (2, 4), (2, 2), (2, 3, 4), (3,), (4,),
+        (), (), (), (2, 4), (8,), (8, 2), (2, 4), (2, 2, 2), (2, 3, 4), (3,), (4,),
         (4,), (2,), (2,), (2,), (), (), (),
     ]
     scratch += [S(sh) if sh else S for sh in shapes]

time: 87.1 us -> 84.3 us (0.968)
  Pallas kernels: 86.2 us -> 82.6 us
    pallas_call x1, Pallas kernels: 84.6 us -> 81.1 us  [body(): pl.pallas_call(kernel, out_shape=(jax.ShapeDtypeStruct((1, 1), F32), jax....]
where the time goes in v5:
time: 84.3 us; the launch traced here: 83.3 us
  Pallas kernels  82.6 us (98%)
    pallas_call x1, Pallas kernels, body(): pl.pallas_call(kernel, out_shape=(jax.ShapeDtypeStruct((1, 1), F32), jax....  81.1 us

profile of v5, /device:TPU:2, one launch (start us, length us, event | category | flops | bytes accessed | tf_op | source)
XLA Modules:
  0.0 83.3 jit_solution(7116970601907626272)
XLA Ops:
  0.6 81.1 %shard_map.84 = (f32[1,1]{1,0:T(1,128)}, f32[64,1024]{1,0:T(8,128)S(1)}, f32[1,1024]{1,0:T(1,128)S(1)}, bf16[256,1024]{1,0:T(8,128)(2,1)S(1)}) custom-call(bf16[256,1024]{1,0:T(8,128)(2,1)} %hid.1, f32[1,1024]{1,0:T(1,128)} %bitcast.5, bf16[64,1024]{1,0:T(8,128)(2,1)} %hin_hbm.1, s32[2,128]{1,0:T(2,128)} %bitcast.6, s32[2,128]{1,0:T(2,128)} %bitcast.7), custom_call_target="tpu_custom_call" | custom-call | tf_op jit(solution)/shard_map/pallas_call | solution.py:765
  81.7 1.6 %shard_map.85 = (f32[1,1]{1,0:T(1,128)}, f32[64,1024]{1,0:T(8,128)}, f32[1,1024]{1,0:T(1,128)}, bf16[256,1024]{1,0:T(8,128)(2,1)}) custom-call(f32[1,1]{1,0:T(1,128)} %get-tuple-element.12.refs_0_, f32[64,1024]{1,0:T(8,128)S(1)} %get-tuple-element.13.refs_1_, f32[1,1024]{1,0:T(1,128)S(1)} %get-tuple-element.14.refs_2_, ...), custom_call_target="tpu_custom_call" | custom-call | tf_op jit(solution)/shard_map/pallas_call | solution.py:783

commit v6 on v5

--- a/solution.py
+++ b/solution.py
@@ -18,15 +18,15 @@
 PEERS = ((1, 0), (3, 0), (2, 0), (0, 1), (1, 1), (3, 1), (2, 1))
 GATHER = (
     ("xe",), ("by", 1), ("bz", 0, 1, 0), ("bz", 1, 1, 0), ("az", 0, 1), ("az", 1, 1), ("by", 2), ("xo",),
-    ("bz", 0, 1, 1), ("bz", 1, 1, 1), ("bz", 0, 2, 0), ("bz", 1, 2, 0), ("xf", 1), ("xf", 0),
-    ("az", 0, 2), ("az", 1, 2), ("by", 3), ("xs", 1), ("xs", 0), ("ty",), ("bz", 0, 1, 2), ("bz", 1, 1, 2), ("iv", 1),
-    ("nm", 1, 0), ("nm", 1, 1), ("nm", 1, 2), ("nm", 1, 3), ("bz", 0, 2, 1), ("bz", 1, 2, 1), ("nm", 1, 4),
-    ("nm", 1, 5), ("nm", 1, 6), ("nm", 1, 7), ("bz", 0, 3, 0), ("bz", 1, 3, 0), ("az", 0, 3), ("az", 1, 3),
-    ("bz", 0, 1, 3), ("bz", 1, 1, 3), ("bz", 0, 2, 2), ("bz", 1, 2, 2), ("xf", 2), ("bz", 0, 3, 1), ("bz", 1, 3, 1),
-    ("tz", 1), ("xs", 2), ("iv", 0), ("nm", 0, 0), ("nm", 0, 1), ("nm", 0, 2), ("bz", 0, 4, 0), ("bz", 1, 2, 3),
-    ("nm", 0, 3), ("nm", 0, 4), ("nm", 0, 5), ("az", 0, 4), ("bz", 1, 3, 2), ("nm", 0, 6), ("nm", 0, 7), ("lg", 0),
-    ("bz", 0, 2, 3), ("bz", 1, 3, 3), ("lg", 7), ("lg", 1), ("bz", 0, 3, 2), ("bz", 1, 4, 2), ("lg", 6), ("tz", 2),
-    ("lg", 2), ("bz", 0, 4, 1), ("lg", 3), ("bz", 0, 3, 3), ("bz", 1, 4, 3), ("lg", 5), ("lg", 4),
+    ("bz", 0, 1, 1), ("bz", 1, 1, 1), ("bz", 0, 2, 0), ("bz", 1, 2, 0), ("az", 0, 2), ("az", 1, 2), ("by", 3),
+    ("xf", 1), ("xf", 0), ("bz", 0, 1, 2), ("bz", 1, 1, 2), ("bz", 0, 2, 1), ("bz", 1, 2, 1), ("ty",),
+    ("bz", 0, 3, 0), ("bz", 1, 3, 0), ("az", 0, 3), ("az", 1, 3), ("xs", 1), ("xs", 0), ("iv", 1), ("bz", 0, 1, 3),
+    ("bz", 1, 1, 3), ("nm", 1, 0), ("nm", 1, 1), ("nm", 1, 2), ("bz", 0, 2, 2), ("bz", 1, 2, 2), ("nm", 1, 3),
+    ("nm", 1, 4), ("xf", 2), ("bz", 0, 3, 1), ("bz", 1, 3, 1), ("nm", 1, 5), ("nm", 1, 6), ("tz", 1), ("bz", 0, 4, 0),
+    ("bz", 1, 2, 3), ("nm", 1, 7), ("az", 0, 4), ("xs", 2), ("iv", 0), ("nm", 0, 0), ("nm", 0, 1), ("bz", 1, 3, 2),
+    ("bz", 0, 2, 3), ("nm", 0, 2), ("nm", 0, 3), ("nm", 0, 4), ("bz", 1, 3, 3), ("nm", 0, 5), ("nm", 0, 6),
+    ("nm", 0, 7), ("bz", 0, 3, 2), ("bz", 1, 4, 2), ("lg", 0), ("lg", 7), ("lg", 1), ("lg", 6), ("lg", 2),
+    ("bz", 0, 3, 3), ("bz", 0, 4, 1), ("lg", 3), ("bz", 1, 4, 3), ("tz", 2), ("lg", 5), ("lg", 4),
 )
 SCATTER = (
     ("hg", 4), ("ai", 4), ("bc", 0, 4, 0), ("bc", 1, 4, 1), ("hg", 3), ("ai", 3), ("bc", 0, 3, 1), ("ds", 0),
@@ -34,10 +34,10 @@
     ("ds", 2), ("yr", 4), ("bc", 0, 3, 0), ("bc", 1, 3, 1), ("hg", 2), ("ai", 2), ("yr", 3), ("du", 1),
     ("bc", 0, 2, 1), ("hg", 6), ("ai", 6), ("yr", 5), ("bc", 1, 2, 0), ("bc", 0, 3, 2), ("bc", 1, 3, 2), ("ds", 3),
     ("tz", 4), ("a4",), ("du", 2), ("hg", 1), ("ai", 1), ("bc", 0, 2, 0), ("bc", 1, 2, 1), ("hg", 7), ("ai", 7),
-    ("du", 3), ("yr", 2), ("gx",), ("qs",), ("bc", 0, 1, 1), ("bc", 1, 1, 0), ("bc", 0, 2, 2), ("bc", 1, 2, 2),
-    ("xr", 1), ("xr", 2), ("yr", 6), ("ac", 0, 3), ("ac", 1, 3), ("hg", 0), ("ai", 0), ("bc", 0, 1, 0),
-    ("bc", 1, 1, 1), ("yr", 1), ("yr", 7), ("bc", 0, 1, 2), ("bc", 1, 1, 2), ("ac", 0, 2), ("ac", 1, 2), ("yr", 0),
-    ("qt",), ("gy",), ("bf", 0), ("bf", 1), ("al", 0), ("bf", 2), ("gz",), ("al", 1), ("bg",), ("af", 0), ("af", 1),
+    ("du", 3), ("yr", 2), ("gx",), ("qs",), ("bc", 0, 1, 1), ("bc", 1, 1, 0), ("xr", 1), ("xr", 2), ("yr", 6),
+    ("ac", 0, 3), ("ac", 1, 3), ("hg", 0), ("ai", 0), ("bc", 0, 2, 2), ("bc", 1, 2, 2), ("bc", 0, 1, 0),
+    ("bc", 1, 1, 1), ("yr", 1), ("yr", 7), ("ac", 0, 2), ("ac", 1, 2), ("bc", 0, 1, 2), ("bc", 1, 1, 2), ("yr", 0),
+    ("qt",), ("gy",), ("bf", 0), ("bf", 1), ("al", 0), ("al", 1), ("bf", 2), ("gz",), ("bg",), ("af", 0), ("af", 1),
     ("bm",), ("fi",), ("gf",), ("gh",),
 )
 

time: 84.3 us -> 83.9 us (level); the launches traced: 83.3 us -> 83.8 us
  no operation moved by 1% of the time
where the time goes in v6:
time: 83.9 us; the launch traced here: 83.8 us
  Pallas kernels  83.2 us (99%)
    pallas_call x1, Pallas kernels, body(): pl.pallas_call(kernel, out_shape=(jax.ShapeDtypeStruct((1, 1), F32), jax....  81.6 us

profile of v6, /device:TPU:2, one launch (start us, length us, event | category | flops | bytes accessed | tf_op | source)
XLA Modules:
  0.0 83.8 jit_solution(4522697205387366218)
XLA Ops:
  0.6 81.6 %shard_map.84 = (f32[1,1]{1,0:T(1,128)}, f32[64,1024]{1,0:T(8,128)S(1)}, f32[1,1024]{1,0:T(1,128)S(1)}, bf16[256,1024]{1,0:T(8,128)(2,1)S(1)}) custom-call(bf16[256,1024]{1,0:T(8,128)(2,1)} %hid.1, f32[1,1024]{1,0:T(1,128)} %bitcast.5, bf16[64,1024]{1,0:T(8,128)(2,1)} %hin_hbm.1, s32[2,128]{1,0:T(2,128)} %bitcast.6, s32[2,128]{1,0:T(2,128)} %bitcast.7), custom_call_target="tpu_custom_call" | custom-call | tf_op jit(solution)/shard_map/pallas_call | solution.py:765
  82.3 1.6 %shard_map.85 = (f32[1,1]{1,0:T(1,128)}, f32[64,1024]{1,0:T(8,128)}, f32[1,1024]{1,0:T(1,128)}, bf16[256,1024]{1,0:T(8,128)(2,1)}) custom-call(f32[1,1]{1,0:T(1,128)} %get-tuple-element.12.refs_0_, f32[64,1024]{1,0:T(8,128)S(1)} %get-tuple-element.13.refs_1_, f32[1,1024]{1,0:T(1,128)S(1)} %get-tuple-element.14.refs_2_, ...), custom_call_target="tpu_custom_call" | custom-call | tf_op jit(solution)/shard_map/pallas_call | solution.py:783

commit v7 on v6

--- a/solution.py
+++ b/solution.py
@@ -24,9 +24,9 @@
     ("bz", 1, 1, 3), ("nm", 1, 0), ("nm", 1, 1), ("nm", 1, 2), ("bz", 0, 2, 2), ("bz", 1, 2, 2), ("nm", 1, 3),
     ("nm", 1, 4), ("xf", 2), ("bz", 0, 3, 1), ("bz", 1, 3, 1), ("nm", 1, 5), ("nm", 1, 6), ("tz", 1), ("bz", 0, 4, 0),
     ("bz", 1, 2, 3), ("nm", 1, 7), ("az", 0, 4), ("xs", 2), ("iv", 0), ("nm", 0, 0), ("nm", 0, 1), ("bz", 1, 3, 2),
-    ("bz", 0, 2, 3), ("nm", 0, 2), ("nm", 0, 3), ("nm", 0, 4), ("bz", 1, 3, 3), ("nm", 0, 5), ("nm", 0, 6),
-    ("nm", 0, 7), ("bz", 0, 3, 2), ("bz", 1, 4, 2), ("lg", 0), ("lg", 7), ("lg", 1), ("lg", 6), ("lg", 2),
-    ("bz", 0, 3, 3), ("bz", 0, 4, 1), ("lg", 3), ("bz", 1, 4, 3), ("tz", 2), ("lg", 5), ("lg", 4),
+    ("nm", 0, 2), ("nm", 0, 3), ("bz", 0, 2, 3), ("nm", 0, 4), ("bz", 1, 3, 3), ("nm", 0, 5), ("nm", 0, 6),
+    ("nm", 0, 7), ("lg", 0), ("lg", 7), ("lg", 1), ("lg", 6), ("lg", 2), ("lg", 3), ("bz", 0, 3, 2), ("bz", 0, 3, 3),
+    ("tz", 2), ("lg", 5), ("bz", 1, 4, 2), ("bz", 0, 4, 1), ("bz", 1, 4, 3), ("lg", 4),
 )
 SCATTER = (
     ("hg", 4), ("ai", 4), ("bc", 0, 4, 0), ("bc", 1, 4, 1), ("hg", 3), ("ai", 3), ("bc", 0, 3, 1), ("ds", 0),

time: 83.9 us -> 83.1 us (level)
  no operation moved by 1% of the time
where the time goes in v7:
time: 83.1 us; the launch traced here: 83 us
  Pallas kernels  82.4 us (99%)
    pallas_call x1, Pallas kernels, body(): pl.pallas_call(kernel, out_shape=(jax.ShapeDtypeStruct((1, 1), F32), jax....  80.8 us

profile of v7, /device:TPU:2, one launch (start us, length us, event | category | flops | bytes accessed | tf_op | source)
XLA Modules:
  0.0 83.0 jit_solution(11081839247188192520)
XLA Ops:
  0.6 80.8 %shard_map.84 = (f32[1,1]{1,0:T(1,128)}, f32[64,1024]{1,0:T(8,128)S(1)}, f32[1,1024]{1,0:T(1,128)S(1)}, bf16[256,1024]{1,0:T(8,128)(2,1)S(1)}) custom-call(bf16[256,1024]{1,0:T(8,128)(2,1)} %hid.1, f32[1,1024]{1,0:T(1,128)} %bitcast.5, bf16[64,1024]{1,0:T(8,128)(2,1)} %hin_hbm.1, s32[2,128]{1,0:T(2,128)} %bitcast.6, s32[2,128]{1,0:T(2,128)} %bitcast.7), custom_call_target="tpu_custom_call" | custom-call | tf_op jit(solution)/shard_map/pallas_call | solution.py:765
  81.5 1.6 %shard_map.85 = (f32[1,1]{1,0:T(1,128)}, f32[64,1024]{1,0:T(8,128)}, f32[1,1024]{1,0:T(1,128)}, bf16[256,1024]{1,0:T(8,128)(2,1)}) custom-call(f32[1,1]{1,0:T(1,128)} %get-tuple-element.12.refs_0_, f32[64,1024]{1,0:T(8,128)S(1)} %get-tuple-element.13.refs_1_, f32[1,1024]{1,0:T(1,128)S(1)} %get-tuple-element.14.refs_2_, ...), custom_call_target="tpu_custom_call" | custom-call | tf_op jit(solution)/shard_map/pallas_call | solution.py:783
